TPU v7x, 32 devices: a whole 2x2x4 slice. The times are simulated.
32 devices in a mesh: dp: 8 (over z, x), shard: 4 (over y, core).
Axes of the slice: x: 2, y: 2, z: 4, core: 2. Of those that a mesh axis runs over, the one named last changes fastest.
Arguments:
- tokens: bfloat16 [32768, 1024], P(('dp', 'shard')), may hold values from -6 to 6
- cotangent: bfloat16 [32768, 1024], P(('dp', 'shard')), may hold values from -6 to 6
- segment_ids: int32 [32768], P(('dp', 'shard')), may hold values from 0 to 5, as said below
- group_counts: int32 [8], replicated, may hold values from 50 to 400
- master_qkv: float32 [1024, 3072], P('dp', 'shard'), may hold values from -0.1875 to 0.1875
- master_out: float32 [1024, 1024], P('dp', 'shard'), may hold values from -1 to 1
- master_up: float32 [1024, 4096], P('dp', 'shard'), may hold values from -0.1875 to 0.1875
- master_down: float32 [4096, 1024], P('dp', 'shard'), may hold values from -0.09375 to 0.09375
- moment_qkv: float32 [1024, 3072], P('dp', 'shard')
- moment_out: float32 [1024, 1024], P('dp', 'shard')
- moment_up: float32 [1024, 4096], P('dp', 'shard')
- moment_down: float32 [4096, 1024], P('dp', 'shard')
- square_qkv: float32 [1024, 3072], P('dp', 'shard'), as said below
- square_out: float32 [1024, 1024], P('dp', 'shard'), as said below
- square_up: float32 [1024, 4096], P('dp', 'shard'), as said below
- square_down: float32 [4096, 1024], P('dp', 'shard'), as said below
- norm_params: float32 [4, 1024], replicated, as said below
- norm_moment: float32 [4, 1024], replicated
- norm_square: float32 [4, 1024], replicated, as said below
Outputs:
- block_out: bfloat16 [32768, 1024], P(('dp', 'shard'))
- input_grad: float32 [32768, 1024], P(('dp', 'shard'))
- grad_qkv: float32 [1024, 3072], P('dp', 'shard')
- grad_out: float32 [1024, 1024], P('dp', 'shard')
- grad_up: float32 [1024, 4096], P('dp', 'shard')
- grad_down: float32 [4096, 1024], P('dp', 'shard')
- new_qkv: float32 [1024, 3072], P('dp', 'shard')
- new_out: float32 [1024, 1024], P('dp', 'shard')
- new_up: float32 [1024, 4096], P('dp', 'shard')
- new_down: float32 [4096, 1024], P('dp', 'shard')
- new_moment_qkv: float32 [1024, 3072], P('dp', 'shard')
- new_moment_out: float32 [1024, 1024], P('dp', 'shard')
- new_moment_up: float32 [1024, 4096], P('dp', 'shard')
- new_moment_down: float32 [4096, 1024], P('dp', 'shard')
- new_square_qkv: float32 [1024, 3072], P('dp', 'shard')
- new_square_out: float32 [1024, 1024], P('dp', 'shard')
- new_square_up: float32 [1024, 4096], P('dp', 'shard')
- new_square_down: float32 [4096, 1024], P('dp', 'shard')
- copy_qkv: bfloat16 [1024, 3072], P('dp', 'shard')
- copy_out: bfloat16 [1024, 1024], P('dp', 'shard')
- copy_up: bfloat16 [1024, 4096], P('dp', 'shard')
- copy_down: bfloat16 [4096, 1024], P('dp', 'shard')
- norm_grad: float32 [4, 1024], replicated
- new_norm: float32 [4, 1024], replicated
- new_norm_moment: float32 [4, 1024], replicated
- new_norm_square: float32 [4, 1024], replicated
Inputs may be any that keep to these rules, and one draw needn't show every extreme that they name: `segment_ids`: in each packed row of 256 tokens the ids number whole images in order, with the padding tokens as one more id placed before, between or after whole images; every row of one group holds images of 50 tokens or every row holds images of 145 tokens, and both kinds of group occur. `norm_params`: gains near one, shifts near zero. `norm_square`: every entry positive. `square_qkv`: every entry positive. `square_out`: every entry positive. `square_up`: every entry positive. `square_down`: every entry positive.
All inputs are finite; a program needn't handle non-finite values.
Results may differ from a plain program's by a relative error of at most 0.012.
Values may be sent and summed in bfloat16 or wider, within the bound.
No kernel may reach another device: no remote copies, remote signals or barrier semaphores. Data moves between devices by JAX's collectives and lax.ppermute only.
A program may use at most 256 MiB of HBM per device.

v0:
```python
import math

import jax
import jax.numpy as jnp
from jax import lax
from jax.sharding import PartitionSpec as P

D = 1024
HEADS = 16
HD = 64
SEQ = 256
STEP = 3


NORM_EPSILON = 1e-06
BETA_FIRST = 0.5
BETA_SECOND = 0.5
ADAM_EPSILON = 1e-08
RATE_MATRIX = 0.02
RATE_OUTPUT = 0.1
RATE_NORMS = 0.3
WEIGHT_DECAY = 0.01
MASK_FILL = -1000000000.0
TRANSPOSED = (((1,), (1,)), ((), ()))
LEADING = (((0,), (0,)), ((), ()))


def layer_norm(values, scales, shifts):
    centred = values - jnp.mean(values, axis=-1, keepdims=True)
    variance = jnp.mean(centred * centred, axis=-1, keepdims=True)
    return centred * lax.rsqrt(variance + NORM_EPSILON) * scales + shifts


def gelu_exact(values):
    return jax.nn.gelu(values, approximate=False)


def adam_update(master, moment, square, gradient, rate):
    new_moment = BETA_FIRST * moment + (1.0 - BETA_FIRST) * gradient
    new_square = BETA_SECOND * square + (1.0 - BETA_SECOND) * gradient * gradient
    bias_first = 1.0 - BETA_FIRST**STEP
    bias_second = 1.0 - BETA_SECOND**STEP
    update = new_moment / bias_first / (jnp.sqrt(new_square / bias_second) + ADAM_EPSILON)
    new_master = master - rate * (update + WEIGHT_DECAY * master)
    return (new_master, new_moment, new_square)


def local(
    tokens,
    cotangent,
    segment_ids,
    group_counts,
    master_qkv,
    master_out,
    master_up,
    master_down,
    moment_qkv,
    moment_out,
    moment_up,
    moment_down,
    square_qkv,
    square_out,
    square_up,
    square_down,
    norm_params,
    norm_moment,
    norm_square,
):
    published = (
        lax.all_gather(master_qkv.astype(jnp.bfloat16), "dp", axis=0, tiled=True),
        lax.all_gather(master_out.astype(jnp.bfloat16), "dp", axis=0, tiled=True),
        lax.all_gather(master_up.astype(jnp.bfloat16), "dp", axis=0, tiled=True),
        lax.all_gather(master_down.astype(jnp.bfloat16), "dp", axis=0, tiled=True),
    )

    def project(activations, position):
        return jnp.dot(
            activations,
            lax.all_gather(published[position], "shard", axis=1, tiled=True),
            preferred_element_type=jnp.float32,
        )

    def project_back(gradient, position):
        return lax.dot_general(
            gradient,
            lax.all_gather(published[position], "shard", axis=1, tiled=True),
            TRANSPOSED,
            preferred_element_type=jnp.float32,
        )

    scaling = 1.0 / math.sqrt(HD)
    inputs = tokens.astype(jnp.float32)
    token_count = inputs.shape[0]
    packed = token_count // SEQ
    normed_one, norm_one_pull = jax.vjp(layer_norm, inputs, norm_params[0], norm_params[1])
    first_in = normed_one.astype(jnp.bfloat16)
    joined = project(first_in, 0).astype(jnp.bfloat16).reshape(packed, SEQ, 3, HEADS, HD)
    query_rows = joined[:, :, 0]
    key_rows = joined[:, :, 1]
    value_rows = joined[:, :, 2]
    segments = segment_ids.reshape(packed, SEQ)
    same_image = (segments[:, :, None] == segments[:, None, :])[:, None]

    def masked_scores():
        raw_scores = (
            jnp.einsum("rqhd,rkhd->rhqk", query_rows, key_rows, preferred_element_type=jnp.float32)
            * scaling
        )
        return jnp.where(same_image, raw_scores, MASK_FILL)

    scores = masked_scores()
    row_max = jnp.max(scores, axis=-1, keepdims=True)
    log_total = row_max + jnp.log(jnp.sum(jnp.exp(scores - row_max), axis=-1, keepdims=True))
    attn_probs = jnp.exp(scores - log_total)
    mixed_heads = jnp.einsum(
        "rhqk,rkhd->rqhd",
        attn_probs.astype(jnp.bfloat16),
        value_rows,
        preferred_element_type=jnp.float32,
    )
    mixed_heads = mixed_heads.reshape(token_count, HEADS * HD).astype(jnp.bfloat16)
    attention = project(mixed_heads, 1)
    residual = inputs + attention
    normed_two, norm_two_pull = jax.vjp(layer_norm, residual, norm_params[2], norm_params[3])
    second_in = normed_two.astype(jnp.bfloat16)
    upward = project(second_in, 2)
    hidden_full, gelu_pull = jax.vjp(gelu_exact, upward)
    hidden = hidden_full.astype(jnp.bfloat16)
    block_out = (residual + project(hidden, 3)).astype(jnp.bfloat16)
    grad_hidden = project_back(cotangent, 3)
    grad_upward = gelu_pull(grad_hidden)[0].astype(jnp.bfloat16)
    grad_second = project_back(grad_upward, 2)
    grad_resid_part, grad_gain_two, grad_shift_two = norm_two_pull(grad_second)
    grad_residual = cotangent.astype(jnp.float32) + grad_resid_part
    grad_attention = grad_residual.astype(jnp.bfloat16)
    grad_mixed = (
        project_back(grad_attention, 1).astype(jnp.bfloat16).reshape(packed, SEQ, HEADS, HD)
    )
    probs_again = jnp.exp(masked_scores() - log_total)
    grad_probs = jnp.einsum(
        "rqhd,rkhd->rhqk", grad_mixed, value_rows, preferred_element_type=jnp.float32
    )
    row_delta = jnp.sum(probs_again * grad_probs, axis=-1, keepdims=True)
    grad_scores = (probs_again * (grad_probs - row_delta)).astype(jnp.bfloat16)
    grad_query = (
        jnp.einsum("rhqk,rkhd->rqhd", grad_scores, key_rows, preferred_element_type=jnp.float32)
        * scaling
    )
    grad_key = (
        jnp.einsum("rhqk,rqhd->rkhd", grad_scores, query_rows, preferred_element_type=jnp.float32)
        * scaling
    )
    grad_value = jnp.einsum(
        "rhqk,rqhd->rkhd",
        probs_again.astype(jnp.bfloat16),
        grad_mixed,
        preferred_element_type=jnp.float32,
    )
    grad_joined = jnp.stack([grad_query, grad_key, grad_value], axis=2).reshape(token_count, 3 * D)
    grad_joined = grad_joined.astype(jnp.bfloat16)
    grad_first = project_back(grad_joined, 0)
    grad_in_part, grad_gain_one, grad_shift_one = norm_one_pull(grad_first)
    input_grad = grad_residual + grad_in_part
    counts = group_counts.astype(jnp.float32)
    own_count = jnp.sum(jnp.where(jnp.arange(counts.shape[0]) == lax.axis_index("dp"), counts, 0.0))
    factor = own_count * counts.shape[0] / jnp.sum(counts)

    def reduce_rows(activations, gradient):
        return lax.psum_scatter(
            factor
            * lax.dot_general(activations, gradient, LEADING, preferred_element_type=jnp.float32),
            "dp",
            scatter_dimension=0,
            tiled=True,
        )

    rows_qkv = reduce_rows(first_in, grad_joined)
    rows_out = reduce_rows(mixed_heads, grad_attention)
    rows_up = reduce_rows(second_in, grad_upward)
    rows_down = reduce_rows(hidden, cotangent)
    owned = (
        lax.psum_scatter(rows_qkv, "shard", scatter_dimension=1, tiled=True),
        lax.psum_scatter(rows_out, "shard", scatter_dimension=1, tiled=True),
        lax.psum_scatter(rows_up, "shard", scatter_dimension=1, tiled=True),
        lax.psum_scatter(rows_down, "shard", scatter_dimension=1, tiled=True),
    )
    grad_qkv = owned[0]
    grad_out = owned[1]
    grad_up = owned[2]
    grad_down = owned[3]
    norm_terms = jnp.stack([grad_gain_one, grad_shift_one, grad_gain_two, grad_shift_two]) * factor
    norm_grad = lax.psum(norm_terms, ("dp", "shard"))
    new_qkv, new_moment_qkv, new_square_qkv = adam_update(
        master_qkv, moment_qkv, square_qkv, grad_qkv, RATE_MATRIX
    )
    new_out, new_moment_out, new_square_out = adam_update(
        master_out, moment_out, square_out, grad_out, RATE_OUTPUT
    )
    new_up, new_moment_up, new_square_up = adam_update(
        master_up, moment_up, square_up, grad_up, RATE_MATRIX
    )
    new_down, new_moment_down, new_square_down = adam_update(
        master_down, moment_down, square_down, grad_down, RATE_MATRIX
    )
    new_norm, new_norm_moment, new_norm_square = adam_update(
        norm_params, norm_moment, norm_square, norm_grad, RATE_NORMS
    )
    return (
        block_out,
        input_grad,
        grad_qkv,
        grad_out,
        grad_up,
        grad_down,
        new_qkv,
        new_out,
        new_up,
        new_down,
        new_moment_qkv,
        new_moment_out,
        new_moment_up,
        new_moment_down,
        new_square_qkv,
        new_square_out,
        new_square_up,
        new_square_down,
        new_qkv.astype(jnp.bfloat16),
        new_out.astype(jnp.bfloat16),
        new_up.astype(jnp.bfloat16),
        new_down.astype(jnp.bfloat16),
        norm_grad,
        new_norm,
        new_norm_moment,
        new_norm_square,
    )


def solution(mesh):
    in_specs = (
        P(("dp", "shard"), None),
        P(("dp", "shard"), None),
        P(("dp", "shard")),
        P(),
        P("dp", "shard"),
        P("dp", "shard"),
        P("dp", "shard"),
        P("dp", "shard"),
        P("dp", "shard"),
        P("dp", "shard"),
        P("dp", "shard"),
        P("dp", "shard"),
        P("dp", "shard"),
        P("dp", "shard"),
        P("dp", "shard"),
        P("dp", "shard"),
        P(),
        P(),
        P(),
    )
    out_specs = (
        P(("dp", "shard"), None),
        P(("dp", "shard"), None),
        P("dp", "shard"),
        P("dp", "shard"),
        P("dp", "shard"),
        P("dp", "shard"),
        P("dp", "shard"),
        P("dp", "shard"),
        P("dp", "shard"),
        P("dp", "shard"),
        P("dp", "shard"),
        P("dp", "shard"),
        P("dp", "shard"),
        P("dp", "shard"),
        P("dp", "shard"),
        P("dp", "shard"),
        P("dp", "shard"),
        P("dp", "shard"),
        P("dp", "shard"),
        P("dp", "shard"),
        P("dp", "shard"),
        P("dp", "shard"),
        P(),
        P(),
        P(),
        P(),
    )
    return jax.shard_map(local, mesh=mesh, in_specs=in_specs, out_specs=out_specs, check_vma=False)
```

profile of v0, /device:TPU:0, one launch (start us, length us, event | category | flops | bytes accessed | tf_op | source)
XLA Modules:
  0.0 1438.0 jit_solution(5193646362434235842)
XLA Ops:
  9.1 1.8 convert_element_type.87
  10.9 1.8 convert_element_type.89
  12.8 45.0 %all-gather.8.cloned.1.call-done = bf16[1024,768]{1,0:T(8,128)(2,1)} async-done(((bf16[128,768]{1,0:T(8,128)(2,1)}), bf16[1024,768]{1,0:T(8,128)(2,1)}) %all-gather.8.cloned.1.call-update) | async-done | bytes 1572880 | tf_op jit(solution)/shard_map/all_gather | solution.py:70
  57.8 34.1 %all_gather.30 = bf16[1024,256]{1,0:T(8,128)(2,1)} all-gather(bf16[128,256]{1,0:T(8,128)(2,1)S(1)} %convert_element_type.85), channel_id=1, replica_groups=mesh['dp'=8,'shard'=4] {'dp'}, dimensions={0}, use_global_device_ids=true | all-gather | bytes 589824 | tf_op jit(solution)/shard_map/all_gather | solution.py:71
  92.0 18.0 %all-gather.14.cloned.1.call-done = bf16[1024,1024]{1,0:T(8,128)(2,1)} async-done(((bf16[128,1024]{1,0:T(8,128)(2,1)}), bf16[1024,1024]{1,0:T(8,128)(2,1)}) %all-gather.14.cloned.1.call-update) | async-done | bytes 2097168 | tf_op jit(solution)/shard_map/all_gather | solution.py:72
  110.1 50.8 %all-gather.18.cloned.1.call-done = bf16[4096,256]{1,0:T(8,128)(2,1)} async-done(((bf16[512,256]{1,0:T(8,128)(2,1)}), bf16[4096,256]{1,0:T(8,128)(2,1)}) %all-gather.18.cloned.1.call-update) | async-done | bytes 2097168 | tf_op jit(solution)/shard_map/all_gather | solution.py:73
  161.0 2.9 copy.63
  163.9 4.7 copy.71
  172.4 34.8 %all-gather.10.cloned.1.call-done = bf16[1024,3072]{1,0:T(8,128)(2,1)} async-done(((bf16[1024,768]{1,0:T(8,128)(2,1)}), bf16[1024,3072]{1,0:T(8,128)(2,1)}) %all-gather.10.cloned.1.call-update) | async-done | bytes 6291472 | tf_op jit(solution)/shard_map/all_gather | solution.py:79
  207.2 12.0 convolution_convert_fusion
  219.2 16.0 %reshape.149 = bf16[4,256,3,16,64]{4,3,2,1,0:T(8,128)(2,1)} reshape(bf16[1024,3072]{1,0:T(8,128)(2,1)} %convolution_convert_fusion) | data formatting | bytes 12582912 | tf_op jit(solution)/shard_map/reshape | solution.py:97
  235.2 10.6 fusion.66
  245.8 5.8 copy.95
  251.7 5.8 copy.94
  257.5 6.0 copy.96
  263.5 10.8 fusion.6
  274.3 10.5 exponential_reduce_fusion
  284.8 10.4 convert_bitcast_fusion.1
  295.2 2.2 copy.69
  297.4 1.9 copy.97
  299.2 5.5 fusion.68
  304.8 2.0 copy-done.5
  307.3 17.1 %fusion.54 = f32[1024,4096]{1,0:T(8,128)} fusion(bf16[1024,4096]{1,0:T(8,128)(2,1)} %all-gather.16.cloned.1.call-done, f32[1024,1024]{0,1:T(8,128)} %copy-done.5, f32[1024]{0:T(1024)S(1)} %bitcast.101, f32[1024]{0:T(1024)S(1)} %bitcast.94, f32[1024]{0:T(1024)S(1)} %fusion.46, f32[1024]{0:T(1024)S(1)} %broadcast_multiply_fusion), kind=kOutput, calls=%fused_computation.111 | convolution fusion | flops 8595177472 | bytes 29376512 | tf_op jit(solution)/shard_map/dot_general | solution.py:77
  324.5 27.7 %all-gather.20.cloned.1.call-done = bf16[4096,1024]{1,0:T(8,128)(2,1)} async-done(((bf16[4096,256]{1,0:T(8,128)(2,1)}), bf16[4096,1024]{1,0:T(8,128)(2,1)}) %all-gather.20.cloned.1.call-update) | async-done | bytes 8388624 | tf_op jit(solution)/shard_map/all_gather | solution.py:79
  352.2 49.8 %add_convert_fusion = (bf16[1024,4096]{1,0:T(8,128)(2,1)S(1)}, f32[1024,4096]{1,0:T(8,128)}) fusion(f32[1024,4096]{1,0:T(8,128)} %fusion.54, bf16[1024,1024]{1,0:T(8,128)(2,1)S(1)} %copy-done.20, bf16[4096,1024]{1,0:T(8,128)(2,1)} %all-gather.20.cloned.1.call-done), kind=kOutput, calls=%fused_computation.4 | convolution fusion | flops 8891924480 | bytes 52428800 | tf_op jit(solution)/shard_map/dot_general | solution.py:84
  402.0 11.1 fusion.69
  413.1 5.7 copy.72
  418.8 5.4 multiply_reduce_fusion.1
  429.2 4.4 convolution_multiply_fusion.3
  433.6 4.6 convolution_convert_fusion.1
  438.2 4.0 reshape.150
  442.3 6.0 copy.74
  448.3 12.7 multiply_reduce_fusion
  461.0 13.0 multiply_convert_fusion
  474.1 4.0 fusion.34
  478.1 2.9 fusion.31
  481.0 11.0 convert_bitcast_fusion
  492.0 3.6 pad_maximum_fusion
  495.6 8.9 copy.79
  504.6 5.0 copy.98
  509.6 2.6 copy-done.17
  512.2 9.3 convolution_multiply_fusion.2
  522.2 16.6 %convolution_multiply_fusion.1 = f32[1024,4096]{1,0:T(8,128)} fusion(bf16[1024,4096]{1,0:T(8,128)(2,1)} %copy-done.59, f32[]{:T(128)S(6)} %div.94, f32[1024,1024]{0,1:T(8,128)} %copy-done.5, f32[1024]{0:T(1024)S(1)} %bitcast.102, f32[1024]{0:T(1024)S(1)} %bitcast.97, f32[1024]{0:T(1024)S(1)} %copy-done.45, f32[1024]{0:T(1024)S(1)} %copy-done.37), kind=kOutput, calls=%fused_computation.24 | convolution fusion | flops 8599371776 | bytes 29376516 | tf_op jit(solution)/shard_map/dot_general | solution.py:171
  538.9 11.9 multiply_convert_fusion.1
  550.8 3.2 copy-done.16
  554.1 11.6 convolution_multiply_fusion
  566.3 166.6 %reduce-scatter.9.cloned.1.call-done = f32[128,3072]{1,0:T(8,128)} async-done(((f32[1024,3072]{1,0:T(8,128)}), f32[128,3072]{1,0:T(8,128)}) %reduce-scatter.9.cloned.1.call-update) | async-done | bytes 1572880 | tf_op jit(solution)/shard_map/reduce_scatter | solution.py:169
  732.9 285.8 %reduce-scatter.17.cloned.1.call-done = f32[128,4096]{1,0:T(8,128)} async-done(((f32[1024,4096]{1,0:T(8,128)}), f32[128,4096]{1,0:T(8,128)}) %reduce-scatter.17.cloned.1.call-update) | async-done | bytes 2097168 | tf_op jit(solution)/shard_map/reduce_scatter | solution.py:169
  1018.8 15.6 %add_convert_fusion.1 = bf16[1024,1024]{0,1:T(8,128)(2,1)} fusion(f32[1024,1024]{0,1:T(8,128)} %copy-done.5, bf16[1024,4096]{1,0:T(8,128)(2,1)} %copy-done.16, bf16[4096,1024]{1,0:T(8,128)(2,1)} %all-gather.20.cloned.1.call-done), kind=kOutput, calls=%fused_computation.51 | convolution fusion | flops 8592031744 | bytes 23068672 | tf_op jit(solution)/shard_map/dot_general | solution.py:77
  1034.4 3.9 copy.83
  1038.3 265.9 %reduce-scatter.21.cloned.1.call-done = f32[512,1024]{1,0:T(8,128)} async-done(((f32[4096,1024]{1,0:T(8,128)}), f32[512,1024]{1,0:T(8,128)}) %reduce-scatter.21.cloned.1.call-update) | async-done | bytes 2097168 | tf_op jit(solution)/shard_map/reduce_scatter | solution.py:169
  1304.3 12.6 fusion.70
  1316.9 5.3 copy.80
  1322.2 3.0 fusion.18
  1325.7 2.7 fusion.16
  1328.4 3.6 add_add_fusion.2
  1332.0 5.8 copy.84
  1339.3 39.4 %psum.7 = f32[4,1024]{1,0:T(4,128)} all-reduce(f32[4,1024]{1,0:T(4,128)} %maximum_multiply_fusion), channel_id=1, replica_groups=mesh['dp'=8,'shard'=4] {'dp','shard'}, use_global_device_ids=true, to_apply=%region_25.26 | all-reduce | flops 4096 | bytes 32768 | tf_op jit(solution)/shard_map/psum | solution.py:192
  1380.1 1.9 fusion.60
  1382.0 2.5 fusion.62
  1384.5 9.6 reduce-scatter.19.cloned.1.call-done
  1394.1 2.5 fusion.58
  1396.7 31.8 %reduce-scatter.23.cloned.1.call-done = f32[512,256]{1,0:T(8,128)} async-done(((f32[512,1024]{1,0:T(8,128)}), f32[512,256]{1,0:T(8,128)}) %reduce-scatter.23.cloned.1.call-update) | async-done | bytes 524304 | tf_op jit(solution)/shard_map/reduce_scatter | solution.py:185
  1428.5 2.5 fusion.56
  (174 shorter events, 15.0 us)
Async XLA Ops:
  7.2 50.6 %copy-start.31 = (f32[128,256]{1,0:T(8,128)S(1)}, f32[128,256]{1,0:T(8,128)}, u32[]{:S(2)}) copy-start(f32[128,256]{1,0:T(8,128)} %param.24) | copy-start | bytes 393220
  7.2 50.5 %all-gather.8.cloned.1.call-start = ((), (), s32[]{:S(2)}) async-start(), calls=%async_computation.8 | async-start | bytes 1769472 | tf_op jit(solution)/shard_map/all_gather | solution.py:70
  9.0 101.0 %all-gather.14.cloned.1.call-start = ((), (), s32[]{:S(2)}) async-start(), calls=%async_computation.11 | async-start | bytes 2359296 | tf_op jit(solution)/shard_map/all_gather | solution.py:72
  10.8 150.1 %copy-start.52 = (s32[1024]{0:T(1024)S(1)}, s32[1024]{0:T(1024)}, u32[]{:S(2)}) copy-start(s32[1024]{0:T(1024)} %param.21) | copy-start | bytes 12292
  10.9 150.0 %all-gather.18.cloned.1.call-start = ((), (), s32[]{:S(2)}) async-start(), calls=%async_computation.13 | async-start | bytes 2359296 | tf_op jit(solution)/shard_map/all_gather | solution.py:73
  12.7 194.5 %all-gather.10.cloned.1.call-start = ((), (), s32[]{:S(2)}) async-start(), calls=%async_computation.9 | async-start | bytes 7864320 | tf_op jit(solution)/shard_map/all_gather | solution.py:79
  57.7 241.5 %all-gather.12.cloned.1.call-start = ((), (), s32[]{:S(2)}) async-start(), calls=%async_computation.10 | async-start | bytes 2621440 | tf_op jit(solution)/shard_map/all_gather | solution.py:79
  91.9 215.4 %all-gather.16.cloned.1.call-start = ((), (), s32[]{:S(2)}) async-start(), calls=%async_computation.12 | async-start | bytes 10485760 | tf_op jit(solution)/shard_map/all_gather | solution.py:79
  110.0 242.2 %all-gather.20.cloned.1.call-start = ((), (), s32[]{:S(2)}) async-start(), calls=%async_computation.14 | async-start | bytes 10485760 | tf_op jit(solution)/shard_map/all_gather | solution.py:79
  160.9 404.8 %reduce-scatter.13.cloned.1.call-start = ((), (), s32[]{:S(2)}) async-start(), calls=%async_computation.17 | async-start | bytes 4718592 | tf_op jit(solution)/shard_map/reduce_scatter | solution.py:169
  161.0 7.6 copy-start.57
  163.8 135.4 %copy-start = (bf16[1024,1024]{0,1:T(8,128)(2,1)}, bf16[1024,1024]{0,1:T(8,128)(2,1)S(1)}, u32[]{:S(2)}) copy-start(bf16[1024,1024]{0,1:T(8,128)(2,1)S(1)} %copy.63) | copy-start | bytes 6291460
  163.9 8.2 copy-start.34
  170.9 48.3 %copy-start.32 = (f32[1024]{0:T(1024)}, f32[1024]{0:T(1024)S(1)}, u32[]{:S(2)}) copy-start(f32[1024]{0:T(1024)S(1)} %broadcast_multiply_fusion.1) | copy-start | bytes 12292
  172.1 47.1 %copy-start.40 = (f32[1024]{0:T(1024)}, f32[1024]{0:T(1024)S(1)}, u32[]{:S(2)}) copy-start(f32[1024]{0:T(1024)S(1)} %fusion.45) | copy-start | bytes 12292
  172.1 47.1 %copy-start.38 = (f32[1,1024]{1,0:T(1,128)}, f32[1,1024]{1,0:T(1,128)S(1)}, u32[]{:S(2)}) copy-start(f32[1,1024]{1,0:T(1,128)S(1)} %get-tuple-element.112) | copy-start | bytes 12292
  172.1 47.1 %copy-start.55 = (f32[1,1024]{1,0:T(1,128)}, f32[1,1024]{1,0:T(1,128)S(1)}, u32[]{:S(2)}) copy-start(f32[1,1024]{1,0:T(1,128)S(1)} %get-tuple-element.111) | copy-start | bytes 12292
  172.1 135.2 %copy-start.46 = (f32[1,1024]{1,0:T(1,128)}, f32[1,1024]{1,0:T(1,128)S(1)}, u32[]{:S(2)}) copy-start(f32[1,1024]{1,0:T(1,128)S(1)} %get-tuple-element.110) | copy-start | bytes 12292
  172.1 135.2 %copy-start.53 = (f32[1,1024]{1,0:T(1,128)}, f32[1,1024]{1,0:T(1,128)S(1)}, u32[]{:S(2)}) copy-start(f32[1,1024]{1,0:T(1,128)S(1)} %get-tuple-element.113) | copy-start | bytes 12292
  172.4 112.4 %copy-start.14 = (pred[4,256,256]{1,2,0:T(8,128)(4,1)}, pred[4,256,256]{1,2,0:T(8,128)(4,1)S(1)}, u32[]{:S(2)}) copy-start(pred[4,256,256]{1,2,0:T(8,128)(4,1)S(1)} %broadcast_compare_fusion) | copy-start | bytes 786436
  284.8 10.4 copy-start.25
  304.8 19.7 %copy-start.36 = (f32[1024]{0:T(1024)}, f32[1024]{0:T(1024)S(1)}, u32[]{:S(2)}) copy-start(f32[1024]{0:T(1024)S(1)} %broadcast_multiply_fusion) | copy-start | bytes 12292
  307.3 17.2 %copy-start.50 = (f32[1024]{0:T(1024)}, f32[1024]{0:T(1024)S(1)}, u32[]{:S(2)}) copy-start(f32[1024]{0:T(1024)S(1)} %multiply_reduce_fusion.3) | copy-start | bytes 12292
  307.3 17.2 %copy-start.44 = (f32[1024]{0:T(1024)}, f32[1024]{0:T(1024)S(1)}, u32[]{:S(2)}) copy-start(f32[1024]{0:T(1024)S(1)} %fusion.46) | copy-start | bytes 12292
  307.3 44.9 %copy-start.20 = (bf16[1024,1024]{1,0:T(8,128)(2,1)S(1)}, bf16[1024,1024]{1,0:T(8,128)(2,1)}, u32[]{:S(2)}) copy-start(bf16[1024,1024]{1,0:T(8,128)(2,1)} %param.20) | copy-start | bytes 6291460
  352.2 49.8 %copy-start.58 = (bf16[1024,4096]{1,0:T(8,128)(2,1)S(1)}, bf16[1024,4096]{1,0:T(8,128)(2,1)}, u32[]{:S(2)}) copy-start(bf16[1024,4096]{1,0:T(8,128)(2,1)} %all-gather.16.cloned.1.call-done) | copy-start | bytes 25165828
  402.0 11.1 copy-start.59
  413.1 5.7 copy-start.37
  413.1 5.7 copy-start.45
  413.1 5.7 copy-start.47
  418.8 5.5 copy-start.51
  418.8 5.5 copy-start.6
  418.8 5.9 copy-start.7
  433.6 299.3 %reduce-scatter.9.cloned.1.call-start = ((), (), s32[]{:S(2)}) async-start(), calls=%async_computation.15 | async-start | bytes 14155776 | tf_op jit(solution)/shard_map/reduce_scatter | solution.py:169
  442.3 6.0 copy-start.12
  442.3 6.0 copy-start.15
  442.3 6.0 copy-start.26
  461.0 13.0 copy-start.8
  474.1 4.1 copy-start.9
  504.6 7.6 copy-start.1
  504.6 7.6 copy-start.33
  504.6 7.6 copy-start.39
  504.6 7.6 copy-start.41
  504.6 7.7 copy-start.56
  521.6 497.1 %reduce-scatter.17.cloned.1.call-start = ((), (), s32[]{:S(2)}) async-start(), calls=%async_computation.19 | async-start | bytes 18874368 | tf_op jit(solution)/shard_map/reduce_scatter | solution.py:169
  538.9 765.4 %reduce-scatter.21.cloned.1.call-start = ((), (), s32[]{:S(2)}) async-start(), calls=%async_computation.21 | async-start | bytes 18874368 | tf_op jit(solution)/shard_map/reduce_scatter | solution.py:169
  538.9 15.2 %copy-start.21 = (bf16[1024,1024]{1,0:T(8,128)(2,1)S(1)}, bf16[1024,1024]{1,0:T(8,128)(2,1)}, u32[]{:S(2)}) copy-start(bf16[1024,1024]{1,0:T(8,128)(2,1)} %param.20) | copy-start | bytes 6291460
  550.8 3.3 copy-start.16
  565.6 814.5 %reduce-scatter.15.cloned.1.call-start = ((), (), s32[]{:S(2)}) async-start(), calls=%async_computation.18 | async-start | bytes 655360 | tf_op jit(solution)/shard_map/reduce_scatter | solution.py:183
  566.2 815.8 %reduce-scatter.11.cloned.1.call-start = ((), (), s32[]{:S(2)}) async-start(), calls=%async_computation.16 | async-start | bytes 1966080 | tf_op jit(solution)/shard_map/reduce_scatter | solution.py:182
  732.9 661.2 %reduce-scatter.19.cloned.1.call-start = ((), (), s32[]{:S(2)}) async-start(), calls=%async_computation.20 | async-start | bytes 2621440 | tf_op jit(solution)/shard_map/reduce_scatter | solution.py:184
  1018.7 409.8 %reduce-scatter.23.cloned.1.call-start = ((), (), s32[]{:S(2)}) async-start(), calls=%async_computation.22 | async-start | bytes 2621440 | tf_op jit(solution)/shard_map/reduce_scatter | solution.py:185
  1322.2 3.5 copy-start.2
  1325.3 3.1 copy-start.4
  1325.3 3.1 copy-start.11
  1325.3 3.1 copy-start.43
  1332.0 46.7 %copy-start.35 = (f32[4,1024]{1,0:T(4,128)S(1)}, f32[4,1024]{1,0:T(4,128)}, u32[]{:S(2)}) copy-start(f32[4,1024]{1,0:T(4,128)} %param.35) | copy-start | bytes 49156
  1332.0 50.0 %copy-start.24 = (f32[128,768]{1,0:T(8,128)S(1)}, f32[128,768]{1,0:T(8,128)}, u32[]{:S(2)}) copy-start(f32[128,768]{1,0:T(8,128)} %param.23) | copy-start | bytes 1179652
  1332.0 62.1 %copy-start.18 = (f32[128,1024]{1,0:T(8,128)S(1)}, f32[128,1024]{1,0:T(8,128)}, u32[]{:S(2)}) copy-start(f32[128,1024]{1,0:T(8,128)} %param.25) | copy-start | bytes 1572868
  1332.0 62.1 %copy-start.27 = (f32[128,1024]{1,0:T(8,128)S(1)}, f32[128,1024]{1,0:T(8,128)}, u32[]{:S(2)}) copy-start(f32[128,1024]{1,0:T(8,128)} %param.29) | copy-start | bytes 1572868
  1332.0 62.1 %copy-start.28 = (f32[128,1024]{1,0:T(8,128)S(1)}, f32[128,1024]{1,0:T(8,128)}, u32[]{:S(2)}) copy-start(f32[128,1024]{1,0:T(8,128)} %param.33) | copy-start | bytes 1572868
  1337.8 90.7 %copy-start.19 = (f32[512,256]{1,0:T(8,128)S(1)}, f32[512,256]{1,0:T(8,128)}, u32[]{:S(2)}) copy-start(f32[512,256]{1,0:T(8,128)} %param.26) | copy-start | bytes 1572868
  1337.8 90.7 %copy-start.29 = (f32[512,256]{1,0:T(8,128)S(1)}, f32[512,256]{1,0:T(8,128)}, u32[]{:S(2)}) copy-start(f32[512,256]{1,0:T(8,128)} %param.30) | copy-start | bytes 1572868
  1337.8 90.7 %copy-start.30 = (f32[512,256]{1,0:T(8,128)S(1)}, f32[512,256]{1,0:T(8,128)}, u32[]{:S(2)}) copy-start(f32[512,256]{1,0:T(8,128)} %param.34) | copy-start | bytes 1572868
  (11 other events, 21.6 us)
Sparse Core Ops, SparseCore 0:
  10.8 46.8 all-gather.7
  60.4 49.5 all-gather.13
  112.7 48.1 all-gather.17
  162.3 44.8 all-gather.9
  208.6 22.8 all-gather.11
  232.9 58.2 all-gather.15
  292.8 59.3 all-gather.19
  433.7 87.9 reduce-scatter.12
  525.7 207.1 reduce-scatter.8
  737.0 281.7 reduce-scatter.16
  1022.5 281.6 reduce-scatter.20
  1307.3 20.7 reduce-scatter.14
  1331.2 28.3 reduce-scatter.10
  1362.6 31.4 reduce-scatter.18
  1397.1 31.4 reduce-scatter.22
where the time goes:
time: 1450 us; the launch traced here: 1440 us
  waiting for transfers between devices  937 us (65%)
  matrix products  222 us (15%)
  local copies, waits for them, and re-layouts  113 us (8%)
  other arithmetic  75.7 us (5%)
  blocking collectives  73.5 us (5%)
  between operations  16.4 us (1%)
    reduce_scatter x4, waiting for transfers between devices, reduce_rows(): lax.psum_scatter(factor * lax.dot_general(activations, gradient, LEADING,...  718 us
    dot_general x4, matrix products, project_back(): lax.dot_general(gradient, lax.all_gather(published[position], 'shard', ax...  78.1 us
    all_gather x4, waiting for transfers between devices, project(): lax.all_gather(published[position], 'shard', axis=1, tiled=True)  62.6 us
    unnamed x129, local copies, waits for them, and re-layouts  54.4 us
    all_gather x1, waiting for transfers between devices, local(): lax.all_gather(master_down.astype(jnp.bfloat16), 'dp', axis=0, tiled=True)  50.8 us
    dot_general x4, matrix products, project(): jnp.dot(activations, lax.all_gather(published[position], 'shard', axis=1,...  50.2 us
    all_gather x1, waiting for transfers between devices, local(): lax.all_gather(master_qkv.astype(jnp.bfloat16), 'dp', axis=0, tiled=True)  45 us
    dot_general x4, matrix products, reduce_rows(): lax.dot_general(activations, gradient, LEADING, preferred_element_type=jn...  41.9 us
  transfers between devices with their start and end apart: 15, of which 10 were waited for; matrix products, arithmetic and copies ran while one was open for 22% of the time, Pallas kernels for 0%

commit v1 on v0

--- a/solution.py
+++ b/solution.py
@@ -1,8 +1,11 @@
+import functools
 import math
 
 import jax
 import jax.numpy as jnp
 from jax import lax
+from jax.experimental import pallas as pl
+from jax.experimental.pallas import tpu as pltpu
 from jax.sharding import PartitionSpec as P
 
 D = 1024
@@ -45,7 +48,135 @@
     return (new_master, new_moment, new_square)
 
 
+def coordinates(index_dp, index_shard):
+    return index_dp // 2, index_dp % 2, index_shard // 2, index_shard % 2
+
+
+def links(dp, shard):
+    depth = dp // 2
+    x_pairs = [(i, i ^ 1) for i in range(dp)]
+    y_pairs = [(i, i ^ 2) for i in range(shard)]
+    c_pairs = [(i, i ^ 1) for i in range(shard)]
+
+    def pull(k):
+        return [((i // 2 + k) % depth * 2 + i % 2, i) for i in range(dp)]
+
+    def push(k):
+        return [(i, j) for j, i in pull(k)]
+
+    return depth, x_pairs, y_pairs, c_pairs, pull, push
+
+
+def gather_pieces(piece, dp, shard):
+    depth, x_pairs, y_pairs, c_pairs, pull, _ = links(dp, shard)
+    half = depth // 2
+    near = jnp.stack([piece] + [lax.ppermute(piece, "dp", pull(k)) for k in range(1, depth)])
+    over_x = lax.ppermute(near, "dp", x_pairs)
+    over_y = lax.ppermute(near, "shard", y_pairs)
+    far_a = lax.ppermute(over_x[:half], "shard", y_pairs)
+    far_b = lax.ppermute(over_y[half:], "dp", x_pairs)
+    mine = [near, over_x, over_y, far_a, far_b]
+    return mine + [lax.ppermute(v, "shard", c_pairs) for v in mine]
+
+
+def piece_places(depth):
+    half = depth // 2
+    places = []
+    for core in (0, 1):
+        base = core * 5
+        places += [(base, k, k, 0, 0, core) for k in range(depth)]
+        places += [(base + 1, k, k, 1, 0, core) for k in range(depth)]
+        places += [(base + 2, k, k, 0, 1, core) for k in range(depth)]
+        places += [(base + 3, k, k, 1, 1, core) for k in range(half)]
+        places += [(base + 4, k - half, k, 1, 1, core) for k in range(half, depth)]
+    return places
+
+
+def assemble(pieces, dp, shard):
+    depth = dp // 2
+    rows, columns = pieces[0].shape[1:]
+    places = piece_places(depth)
+
+    def kernel(*refs):
+        ins, out, sems = refs[:10], refs[10], refs[11]
+        z, x, y, c = coordinates(lax.axis_index("dp"), lax.axis_index("shard"))
+        copies = []
+        for n, (i, j, dz, dx, dy, dc) in enumerate(places):
+            row = (lax.rem(z + dz, depth) * 2 + lax.rem(x + dx, 2)) * rows
+            column = (lax.rem(y + dy, 2) * 2 + lax.rem(c + dc, 2)) * columns
+            target = out.at[pl.ds(pl.multiple_of(row, rows), rows), pl.ds(pl.multiple_of(column, columns), columns)]
+            copies.append(pltpu.make_async_copy(ins[i].at[j], target, sems.at[n]))
+        for copy in copies:
+            copy.start()
+        for copy in copies:
+            copy.wait()
+
+    return pl.pallas_call(
+        kernel,
+        out_shape=jax.ShapeDtypeStruct((rows * dp, columns * shard), pieces[0].dtype),
+        in_specs=[pl.BlockSpec(memory_space=pl.ANY)] * 10,
+        out_specs=pl.BlockSpec(memory_space=pltpu.VMEM),
+        scratch_shapes=[pltpu.SemaphoreType.DMA((len(places),))],
+        compiler_params=pltpu.CompilerParams(vmem_limit_bytes=32 * 2**20),
+    )(*pieces)
+
+
+def spread(whole, dp, shard):
+    depth = dp // 2
+    rows, columns = whole.shape[0] // dp, whole.shape[1] // shard
+    shape = jax.ShapeDtypeStruct((2, 2, depth, rows, columns), whole.dtype)
+
+    def kernel(source, near, far, sems):
+        z, x, y, c = coordinates(lax.axis_index("dp"), lax.axis_index("shard"))
+        copies = []
+        for dc, out in enumerate((near, far)):
+            for dy in range(2):
+                for dx in range(2):
+                    for dz in range(depth):
+                        row = (lax.rem(z + dz, depth) * 2 + lax.rem(x + dx, 2)) * rows
+                        column = (lax.rem(y + dy, 2) * 2 + lax.rem(c + dc, 2)) * columns
+                        block = source.at[pl.ds(pl.multiple_of(row, rows), rows), pl.ds(pl.multiple_of(column, columns), columns)]
+                        copies.append(pltpu.make_async_copy(block, out.at[dy, dx, dz], sems.at[len(copies)]))
+        for copy in copies:
+            copy.start()
+        for copy in copies:
+            copy.wait()
+
+    return pl.pallas_call(
+        kernel,
+        out_shape=(shape, shape),
+        in_specs=[pl.BlockSpec(memory_space=pltpu.VMEM)],
+        out_specs=(pl.BlockSpec(memory_space=pl.ANY),) * 2,
+        scratch_shapes=[pltpu.SemaphoreType.DMA((dp * shard,))],
+        compiler_params=pltpu.CompilerParams(vmem_limit_bytes=32 * 2**20),
+    )(whole)
+
+
+def scatter_pieces(near, far, dp, shard):
+    depth, x_pairs, y_pairs, c_pairs, _, push = links(dp, shard)
+    half = depth // 2
+
+    def wide(v):
+        return v.astype(jnp.float32)
+
+    def thin(v):
+        return v.astype(jnp.bfloat16)
+
+    both = wide(near) + wide(lax.ppermute(far, "shard", c_pairs))
+    far_a = lax.ppermute(thin(both[1, 1, :half]), "shard", y_pairs)
+    far_b = lax.ppermute(thin(both[1, 1, half:]), "dp", x_pairs)
+    for_x = jnp.concatenate([both[0, 1, :half] + wide(far_a), both[0, 1, half:]])
+    for_y = jnp.concatenate([both[1, 0, :half], both[1, 0, half:] + wide(far_b)])
+    here = both[0, 0] + wide(lax.ppermute(thin(for_x), "dp", x_pairs)) + wide(lax.ppermute(thin(for_y), "shard", y_pairs))
+    total = here[0]
+    for k in range(1, depth):
+        total = total + wide(lax.ppermute(thin(here[k]), "dp", push(k)))
+    return total
+
+
 def local(
+    dp,
+    shard,
     tokens,
     cotangent,
     segment_ids,
@@ -66,26 +197,17 @@
     norm_moment,
     norm_square,
 ):
-    published = (
-        lax.all_gather(master_qkv.astype(jnp.bfloat16), "dp", axis=0, tiled=True),
-        lax.all_gather(master_out.astype(jnp.bfloat16), "dp", axis=0, tiled=True),
-        lax.all_gather(master_up.astype(jnp.bfloat16), "dp", axis=0, tiled=True),
-        lax.all_gather(master_down.astype(jnp.bfloat16), "dp", axis=0, tiled=True),
-    )
+    published = [
+        assemble(gather_pieces(w.astype(jnp.bfloat16), dp, shard), dp, shard)
+        for w in (master_qkv, master_out, master_up, master_down)
+    ]
 
     def project(activations, position):
-        return jnp.dot(
-            activations,
-            lax.all_gather(published[position], "shard", axis=1, tiled=True),
-            preferred_element_type=jnp.float32,
-        )
+        return jnp.dot(activations, published[position], preferred_element_type=jnp.float32)
 
     def project_back(gradient, position):
         return lax.dot_general(
-            gradient,
-            lax.all_gather(published[position], "shard", axis=1, tiled=True),
-            TRANSPOSED,
-            preferred_element_type=jnp.float32,
+            gradient, published[position], TRANSPOSED, preferred_element_type=jnp.float32
         )
 
     scaling = 1.0 / math.sqrt(HD)
@@ -165,24 +287,17 @@
     own_count = jnp.sum(jnp.where(jnp.arange(counts.shape[0]) == lax.axis_index("dp"), counts, 0.0))
     factor = own_count * counts.shape[0] / jnp.sum(counts)
 
-    def reduce_rows(activations, gradient):
-        return lax.psum_scatter(
-            factor
-            * lax.dot_general(activations, gradient, LEADING, preferred_element_type=jnp.float32),
-            "dp",
-            scatter_dimension=0,
-            tiled=True,
+    def reduce_whole(activations, gradient):
+        partial = factor * lax.dot_general(
+            activations, gradient, LEADING, preferred_element_type=jnp.float32
         )
-
-    rows_qkv = reduce_rows(first_in, grad_joined)
-    rows_out = reduce_rows(mixed_heads, grad_attention)
-    rows_up = reduce_rows(second_in, grad_upward)
-    rows_down = reduce_rows(hidden, cotangent)
+        return scatter_pieces(*spread(partial.astype(jnp.bfloat16), dp, shard), dp, shard)
+
     owned = (
-        lax.psum_scatter(rows_qkv, "shard", scatter_dimension=1, tiled=True),
-        lax.psum_scatter(rows_out, "shard", scatter_dimension=1, tiled=True),
-        lax.psum_scatter(rows_up, "shard", scatter_dimension=1, tiled=True),
-        lax.psum_scatter(rows_down, "shard", scatter_dimension=1, tiled=True),
+        reduce_whole(first_in, grad_joined),
+        reduce_whole(mixed_heads, grad_attention),
+        reduce_whole(second_in, grad_upward),
+        reduce_whole(hidden, cotangent),
     )
     grad_qkv = owned[0]
     grad_out = owned[1]
@@ -285,4 +400,5 @@
         P(),
         P(),
     )
-    return jax.shard_map(local, mesh=mesh, in_specs=in_specs, out_specs=out_specs, check_vma=False)
+    local_step = functools.partial(local, mesh.shape["dp"], mesh.shape["shard"])
+    return jax.shard_map(local_step, mesh=mesh, in_specs=in_specs, out_specs=out_specs, check_vma=False)

time: 1450 us -> 835 us (0.58)
  waiting for transfers between devices: 937 us -> 228 us
  starting transfers between devices: 0.6 us -> 85.8 us
  blocking collectives: 73.5 us -> 39.6 us
  local copies, waits for them, and re-layouts: 113 us -> 141 us
  Pallas kernels: 0 us -> 17.8 us
  other arithmetic: 75.7 us -> 93 us
    reduce_scatter x8 -> x0, waiting for transfers between devices: 760 us -> none  [the longest x4 718 us: reduce_rows(): lax.psum_scatter(factor * lax.dot_general(activations, gradient, LEADING,...]
    ppermute x0 -> x80, waiting for transfers between devices: none -> 228 us  [the longest x12 43.4 us: gather_pieces(): lax.ppermute(piece, 'dp', pull(k))]
    all_gather x7 -> x0, waiting for transfers between devices: 176 us -> none  [the longest x4 62.6 us: project(): lax.all_gather(published[position], 'shard', axis=1, tiled=True)]
    ppermute x0 -> x80, starting transfers between devices: none -> 85.8 us  [the longest x12 31.3 us: gather_pieces(): lax.ppermute(piece, 'dp', pull(k))]
    all_gather x1 -> x0, blocking collectives: 34.1 us -> none  [local(): lax.all_gather(master_out.astype(jnp.bfloat16), 'dp', axis=0, tiled=True)]
    another operation x0 -> x19, other arithmetic: none -> 29.7 us
    pallas_call x0 -> x8, Pallas kernels: none -> 17.8 us  [the longest x4 10.2 us: assemble(): pl.pallas_call(kernel, out_shape=jax.ShapeDtypeStruct((rows * dp, columns...]
    unnamed x129 -> x205, local copies, waits for them, and re-layouts: 54.4 us -> 66.2 us
  transfers between devices with their start and end apart: 15 -> 80, of which waited for: 10 -> 31; matrix products, arithmetic and copies ran while one was open for 22% -> 20% of each run, Pallas kernels for 0% -> 1%
where the time goes in v1:
time: 835 us; the launch traced here: 821 us
  waiting for transfers between devices  228 us (27%)
  matrix products  212 us (25%)
  local copies, waits for them, and re-layouts  141 us (17%)
  other arithmetic  93 us (11%)
  starting transfers between devices  85.8 us (10%)
  blocking collectives  39.6 us (5%)
  Pallas kernels  17.8 us (2%)
    dot_general x4, matrix products, project(): jnp.dot(activations, published[position], preferred_element_type=jnp.floa...  72.9 us
    unnamed x205, local copies, waits for them, and re-layouts  66.2 us
    dot_general x4, matrix products, project_back(): lax.dot_general(gradient, published[position], TRANSPOSED, preferred_elem...  52 us
    ppermute x12, waiting for transfers between devices, gather_pieces(): lax.ppermute(piece, 'dp', pull(k))  43.4 us
    ppermute x4, waiting for transfers between devices, gather_pieces(): over_x = lax.ppermute(near, 'dp', x_pairs)  41.3 us
    psum x1, blocking collectives, local(): norm_grad = lax.psum(norm_terms, ('dp', 'shard'))  39.6 us
    dot_general x4, matrix products, reduce_whole(): lax.dot_general(activations, gradient, LEADING, preferred_element_type=jn...  36.2 us
    ppermute x4, waiting for transfers between devices, scatter_pieces(): lax.ppermute(thin(for_x), 'dp', x_pairs)  35.6 us
  transfers between devices with their start and end apart: 80, of which 31 were waited for; matrix products, arithmetic and copies ran while one was open for 20% of the time, Pallas kernels for 1%

profile of v1, /device:TPU:0, one launch (start us, length us, event | category | flops | bytes accessed | tf_op | source)
XLA Modules:
  0.0 821.2 jit_solution(4043546411489535247)
XLA Ops:
  1.8 5.1 collective-permute-start
  14.4 7.7 collective-permute-done.12
  22.1 3.4 collective-permute-start.25
  30.4 7.5 collective-permute-start.14
  38.1 13.6 %collective-permute-done.13 = bf16[128,256]{1,0:T(8,128)(2,1)S(1)} collective-permute-done((bf16[128,256]{1,0:T(8,128)(2,1)S(1)}, bf16[128,256]{1,0:T(8,128)(2,1)S(1)}, u32[]{:S(2)}, u32[]{:S(2)}) %collective-permute-start.13) | collective-permute-done | bytes 65568 | tf_op jit(solution)/shard_map/ppermute | solution.py:73
  56.1 19.8 %collective-permute-done.15.refs_1_ = bf16[4,128,256]{2,1,0:T(8,128)(2,1)S(1)} collective-permute-done((bf16[4,128,256]{2,1,0:T(8,128)(2,1)S(1)}, bf16[4,128,256]{2,1,0:T(8,128)(2,1)S(1)}, u32[]{:S(2)}, u32[]{:S(2)}) %collective-permute-start.15) | collective-permute-done | bytes 262176 | tf_op jit(solution)/shard_map/ppermute | solution.py:74
  80.5 22.9 %collective-permute-done.17.refs_3_ = bf16[2,128,256]{2,1,0:T(8,128)(2,1)S(1)} collective-permute-done((bf16[2,128,256]{2,1,0:T(8,128)(2,1)S(1)}, bf16[2,128,256]{2,1,0:T(8,128)(2,1)S(1)}, u32[]{:S(2)}, u32[]{:S(2)}) %collective-permute-start.17) | collective-permute-done | bytes 131104 | tf_op jit(solution)/shard_map/ppermute | solution.py:76
  104.3 4.1 collective-permute-done.18.refs_4_
  110.5 3.9 copy.64
  150.1 9.1 %convolution_convert_fusion = bf16[1024,3072]{1,0:T(8,128)(2,1)} fusion(bf16[1024,3072]{1,0:T(8,128)(2,1)S(1)} %shard_map.386, bf16[1024,1024]{0,1:T(8,128)(2,1)S(1)} %copy-done.17, f32[1024]{0:T(1024)S(1)} %bitcast.327, f32[1024]{0:T(1024)S(1)} %bitcast.318, f32[1024]{0:T(1024)S(1)} %fusion.88, f32[1024]{0:T(1024)S(1)} %broadcast_multiply_fusion.1), kind=kOutput, calls=%fused_computation.48 | convolution fusion | flops 6451888128 | bytes 14696448 | tf_op jit(solution)/shard_map/dot_general | solution.py:206
  159.2 16.0 %reshape.169 = bf16[4,256,3,16,64]{4,3,2,1,0:T(8,128)(2,1)} reshape(bf16[1024,3072]{1,0:T(8,128)(2,1)} %convolution_convert_fusion) | data formatting | bytes 12582912 | tf_op jit(solution)/shard_map/reshape | solution.py:219
  175.2 9.0 %fusion.125 = (bf16[4,256,1,16,64]{4,3,2,1,0:T(8,128)(2,1)}, bf16[4,256,1,16,64]{4,3,2,1,0:T(8,128)(2,1)}, bf16[4,256,1,16,64]{4,3,2,1,0:T(8,128)(2,1)}) fusion(bf16[4,256,3,16,64]{4,3,2,1,0:T(8,128)(2,1)} %reshape.169), kind=kLoop, calls=%fused_computation.229 | loop fusion | bytes 12582912 | tf_op jit(solution)/shard_map/slice | solution.py:220
  184.2 5.8 copy.98
  190.0 6.2 copy.99
  196.2 10.8 %fusion.13 = (f32[4,16,256]{2,1,0:T(8,128)S(1)}, f32[4,16,256,256]{2,3,1,0:T(8,128)}) fusion(pred[4,256,256]{1,2,0:T(8,128)(4,1)S(1)} %copy-done.35, bf16[4,256,1,16,64]{1,4,3,0,2:T(8,128)(2,1)} %copy.99, bf16[4,256,1,16,64]{1,4,3,0,2:T(8,128)(2,1)} %copy.98), kind=kOutput, calls=%fused_computation.32 | convolution fusion | flops 549437440 | bytes 21299200 | tf_op jit(solution)/shard_map/rqhd,rkhd->rhqk/dot_general | solution.py:228
  207.0 10.4 %exponential_reduce_fusion = f32[4,16,256]{2,1,0:T(8,128)S(1)} fusion(f32[4,16,256,256]{2,3,1,0:T(8,128)} %get-tuple-element.188, f32[4,16,256]{2,1,0:T(8,128)S(1)} %get-tuple-element.187, pred[4,256,256]{1,2,0:T(8,128)(4,1)S(1)} %copy-done.35), kind=kLoop, calls=%fused_computation.29 | loop fusion | flops 16760832 | bytes 17170432 | tf_op jit(solution)/shard_map/reduce_sum | solution.py:235
  217.5 6.4 copy.97
  223.9 10.3 %convert_bitcast_fusion.1 = bf16[4,256,16,64]{1,3,2,0:T(8,128)(2,1)S(1)} fusion(bf16[4,256,1,16,64]{1,4,3,0,2:T(8,128)(2,1)} %copy.97, f32[4,16,256,256]{2,3,1,0:T(8,128)} %get-tuple-element.188, f32[4,16,256]{2,1,0:T(8,128)S(1)} %log_add_fusion, pred[4,256,256]{1,2,0:T(8,128)(4,1)S(1)} %copy-done.35), kind=kOutput, calls=%fused_computation.84 | convolution fusion | flops 554696704 | bytes 21299200 | tf_op jit(solution)/shard_map/rhqk,rkhd->rqhd/dot_general | solution.py:237
  245.3 46.0 %multiply_convert_fusion.3 = (bf16[1024,4096]{1,0:T(8,128)(2,1)S(1)}, f32[1024,4096]{1,0:T(8,128)}, f32[1024,4096]{1,0:T(8,128)}) fusion(bf16[1024,4096]{1,0:T(8,128)(2,1)S(1)} %shard_map.388, bf16[1024,1024]{0,1:T(8,128)(2,1)S(1)} %add_convert_fusion.3.clone.4), kind=kOutput, calls=%fused_computation.15 | convolution fusion | flops 8862564352 | bytes 52428800 | tf_op jit(solution)/shard_map/dot_general | solution.py:206
  291.2 3.3 copy-done.93
  294.5 9.6 %multiply_convert_fusion.source = bf16[4096,1024]{1,0:T(8,128)(2,1)S(1)} fusion(bf16[1024,4096]{1,0:T(8,128)(2,1)S(1)} %get-tuple-element.133, bf16[1024,1024]{1,0:T(8,128)(2,1)S(1)} %copy-done.44, f32[]{:T(128)S(6)} %div.94), kind=kOutput, calls=%fused_computation.11 | convolution fusion | flops 8598323200 | bytes 18874372 | tf_op jit(solution)/shard_map/dot_general | solution.py:291
  305.9 7.0 collective-permute-done.72
  315.0 5.5 fusion.98
  324.9 11.3 %collective-permute-done.73 = bf16[2,512,256]{2,1,0:T(8,128)(2,1)S(1)} collective-permute-done((bf16[2,512,256]{2,1,0:T(8,128)(2,1)S(1)}, bf16[2,512,256]{2,1,0:T(8,128)(2,1)S(1)}, u32[]{:S(2)}, u32[]{:S(2)}) %collective-permute-start.73) | collective-permute-done | bytes 524320 | tf_op jit(solution)/shard_map/ppermute | solution.py:166
  339.7 22.2 %collective-permute-done.74 = bf16[4,512,256]{2,1,0:T(8,128)(2,1)S(1)} collective-permute-done((bf16[4,512,256]{2,1,0:T(8,128)(2,1)S(1)}, bf16[4,512,256]{2,1,0:T(8,128)(2,1)S(1)}, u32[]{:S(2)}, u32[]{:S(2)}) %collective-permute-start.74) | collective-permute-done | bytes 1048608 | tf_op jit(solution)/shard_map/ppermute | solution.py:170
  368.2 6.5 collective-permute-done.77
  374.7 8.1 collective-permute-done.78
  384.4 6.2 collective-permute-start.36
  391.2 6.2 collective-permute-done.36
  397.4 15.8 %collective-permute-done.37 = bf16[512,256]{1,0:T(8,128)(2,1)S(1)} collective-permute-done((bf16[512,256]{1,0:T(8,128)(2,1)S(1)}, bf16[512,256]{1,0:T(8,128)(2,1)S(1)}, u32[]{:S(2)}, u32[]{:S(2)}) %collective-permute-start.37) | collective-permute-done | bytes 262176 | tf_op jit(solution)/shard_map/ppermute | solution.py:73
  415.2 21.5 %collective-permute-done.39.refs_1_ = bf16[4,512,256]{2,1,0:T(8,128)(2,1)S(1)} collective-permute-done((bf16[4,512,256]{2,1,0:T(8,128)(2,1)S(1)}, bf16[4,512,256]{2,1,0:T(8,128)(2,1)S(1)}, u32[]{:S(2)}, u32[]{:S(2)}) %collective-permute-start.39) | collective-permute-done | bytes 1048608 | tf_op jit(solution)/shard_map/ppermute | solution.py:74
  439.3 9.6 %collective-permute-done.41.refs_3_ = bf16[2,512,256]{2,1,0:T(8,128)(2,1)} collective-permute-done((bf16[2,512,256]{2,1,0:T(8,128)(2,1)S(1)}, bf16[2,512,256]{2,1,0:T(8,128)(2,1)}, u32[]{:S(2)}, u32[]{:S(2)}) %collective-permute-start.41) | collective-permute-done | bytes 524320 | tf_op jit(solution)/shard_map/ppermute | solution.py:76
  448.9 4.0 collective-permute-done.42.refs_4_
  452.9 4.2 copy.72
  463.6 25.2 %fusion.6 = bf16[1024,4096]{1,0:T(8,128)(2,1)} fusion(f32[1024,4096]{1,0:T(8,128)} %get-tuple-element.134, f32[1024,4096]{1,0:T(8,128)} %get-tuple-element.191, bf16[4096,1024]{1,0:T(8,128)(2,1)} %copy-done.1, bf16[1024,1024]{1,0:T(8,128)(2,1)} %param.20), kind=kOutput, calls=%fused_computation.9 | convolution fusion | flops 8648654848 | bytes 52428800 | tf_op jit(solution)/shard_map/dot_general | solution.py:209
  488.8 15.7 %fusion.128 = (f32[1024]{0:T(1024)}, f32[1024,1024]{1,0:T(8,128)}) fusion(bf16[1024,4096]{1,0:T(8,128)(2,1)} %fusion.6, bf16[1024,4096]{1,0:T(8,128)(2,1)} %copy-done), kind=kOutput, calls=%fused_computation.232 | convolution fusion | flops 8590982144 | bytes 20975616 | tf_op jit(solution)/shard_map/dot_general | solution.py:209
  504.5 5.8 copy.74
  510.3 5.4 multiply_reduce_fusion.1
  523.0 3.9 reshape.170
  527.0 6.0 copy.76
  533.0 12.4 %multiply_reduce_fusion = (f32[4,16,256]{2,1,0:T(8,128)S(1)}, f32[4,16,256,256]{2,3,1,0:T(8,128)}) fusion(f32[4,16,256,256]{2,3,1,0:T(8,128)} %get-tuple-element.188, f32[4,16,256]{2,1,0:T(8,128)S(1)} %copy-done.53, pred[4,256,256]{1,2,0:T(8,128)(4,1)S(1)} %copy-done.36, bf16[4,256,16,64]{1,3,2,0:T(8,128)(2,1)} %copy.76, ...), kind=kOutput, calls=%fused_computation.14 | convolution fusion | flops 557826048 | bytes 38141952 | tf_op jit(solution)/shard_map/rqhd,rkhd->rhqk/dot_general | solution.py:262
  545.4 12.4 %multiply_convert_fusion.2 = bf16[4,16,256,256]{2,3,1,0:T(8,128)(2,1)S(1)} fusion(f32[4,16,256,256]{2,3,1,0:T(8,128)} %get-tuple-element.193, f32[4,16,256,256]{2,3,1,0:T(8,128)} %get-tuple-element.188, f32[4,16,256]{2,1,0:T(8,128)S(1)} %get-tuple-element.192, f32[4,16,256]{2,1,0:T(8,128)S(1)} %copy-done.53, pred[4,256,256]{1,2,0:T(8,128)(4,1)S(1)} %copy-done.36), kind=kLoop, calls=%fused_computation.13 | loop fusion | flops 25165824 | bytes 42336256 | tf_op jit(solution)/shard_map/convert_element_type | solution.py:266
  560.7 4.0 fusion.45
  564.7 11.0 %convert_bitcast_fusion = bf16[4,256,1,16,64]{1,4,3,0,2:T(8,128)(2,1)} fusion(bf16[4,256,16,64]{1,3,2,0:T(8,128)(2,1)S(1)} %copy-done.34, f32[4,16,256,256]{2,3,1,0:T(8,128)} %get-tuple-element.188, f32[4,16,256]{2,1,0:T(8,128)S(1)} %copy-done.53, pred[4,256,256]{1,2,0:T(8,128)(4,1)S(1)} %copy-done.36), kind=kOutput, calls=%fused_computation.83 | convolution fusion | flops 554696704 | bytes 21299200 | tf_op jit(solution)/shard_map/rhqk,rqhd->rkhd/dot_general | solution.py:275
  575.7 15.3 %multiply_convert_fusion.1.source = bf16[1024,4096]{1,0:T(8,128)(2,1)} fusion(bf16[1024,4096]{1,0:T(8,128)(2,1)} %fusion.6, f32[]{:T(128)S(6)} %div.94, f32[1024,1024]{0,1:T(8,128)S(1)} %copy-done.24, f32[1024]{0:T(1024)S(1)} %bitcast.324, f32[1024]{0:T(1024)S(1)} %bitcast.314, f32[1024]{0:T(1024)S(1)} %copy-done.68, f32[1024]{0:T(1024)S(1)} %copy-done.66), kind=kOutput, calls=%fused_computation.12 | convolution fusion | flops 8603566080 | bytes 20987908 | tf_op jit(solution)/shard_map/dot_general | solution.py:291
  593.9 3.4 pad_maximum_fusion
  597.2 11.8 %copy.81 = bf16[4,256,3,16,64]{1,0,4,3,2:T(4,128)(2,1)} copy(bf16[4,256,3,16,64]{1,4,3,0,2:T(8,128)(2,1)} %pad_maximum_fusion) | data formatting | bytes 12582912 | tf_op jit(solution)/shard_map/stack | solution.py:281
  609.0 5.0 copy.101
  614.1 8.8 %fusion.129 = (f32[1024]{0:T(1024)S(1)}, f32[1024,1024]{1,0:T(8,128)}) fusion(bf16[1024,3072]{0,1:T(8,128)(2,1)S(1)} %bitcast.297, bf16[1024,3072]{1,0:T(8,128)(2,1)S(1)} %bitcast.292), kind=kOutput, calls=%fused_computation.233 | convolution fusion | flops 6443498496 | bytes 16781312 | tf_op jit(solution)/shard_map/dot_general | solution.py:209
  622.9 8.9 %multiply_convert_fusion.4.source = bf16[1024,3072]{1,0:T(8,128)(2,1)} fusion(bf16[1024,3072]{0,1:T(8,128)(2,1)S(1)} %bitcast.298, f32[]{:T(128)S(6)} %div.94, bf16[1024,1024]{0,1:T(8,128)(2,1)S(1)} %copy-done.19, f32[1024]{0:T(1024)S(1)} %bitcast.328, f32[1024]{0:T(1024)S(1)} %bitcast.319, f32[1024]{0:T(1024)S(1)} %copy-done.78, f32[1024]{0:T(1024)S(1)} %copy-done.64), kind=kOutput, calls=%fused_computation.33 | convolution fusion | flops 6455033856 | bytes 14696452 | tf_op jit(solution)/shard_map/dot_general | solution.py:291
  631.8 15.3 %add_convert_fusion = bf16[1024,1024]{0,1:T(8,128)(2,1)} fusion(f32[1024,1024]{0,1:T(8,128)} %copy-done.22, bf16[1024,4096]{1,0:T(8,128)(2,1)} %copy-done.93, bf16[4096,1024]{1,0:T(8,128)(2,1)} %copy-done.1), kind=kOutput, calls=%fused_computation.63 | convolution fusion | flops 8592031744 | bytes 23068672 | tf_op jit(solution)/shard_map/dot_general | solution.py:206
  647.2 5.3 copy.82
  652.5 3.4 copy-done.2
  670.8 3.8 collective-permute-done.57
  678.5 3.6 add_add_fusion.2
  682.1 39.6 %psum.7 = f32[4,1024]{1,0:T(4,128)S(1)} all-reduce(f32[4,1024]{1,0:T(4,128)S(1)} %maximum_multiply_fusion), channel_id=1, replica_groups=mesh['dp'=8,'shard'=4] {'dp','shard'}, use_global_device_ids=true, to_apply=%region_17.18 | all-reduce | flops 4096 | bytes 32768 | tf_op jit(solution)/shard_map/psum | solution.py:307
  728.2 5.6 fusion.96
  737.9 6.5 fusion.97
  752.4 7.2 collective-permute-done.65
  766.9 5.7 copy.86
  777.0 3.4 collective-permute-done.50
  788.8 10.0 %collective-permute-done.66 = bf16[4,128,1024]{2,1,0:T(8,128)(2,1)S(1)} collective-permute-done((bf16[4,128,1024]{2,1,0:T(8,128)(2,1)}, bf16[4,128,1024]{2,1,0:T(8,128)(2,1)S(1)}, u32[]{:S(2)}, u32[]{:S(2)}) %collective-permute-start.66) | collective-permute-done | bytes 1048608 | tf_op jit(solution)/shard_map/ppermute | solution.py:170
  807.6 5.0 collective-permute-done.69
  812.6 6.7 collective-permute-done.70
  (416 shorter events, 182.6 us)
Async XLA Ops:
  1.8 23.7 %collective-permute-start = (bf16[128,768]{1,0:T(8,128)(2,1)S(1)}, bf16[128,768]{1,0:T(8,128)(2,1)S(1)}, u32[]{:S(2)}, u32[]{:S(2)}) collective-permute-start(bf16[128,768]{1,0:T(8,128)(2,1)S(1)} %convert_element_type.287), channel_id=1, source_target_pairs={{8,0},{12,4},{16,8},{20,12},{24,16},{28,20},{0,24},{4,28},{9,1},{1... | collective-permute-start | bytes 589832 | tf_op jit(solution)/shard_map/ppermute | solution.py:73
  6.9 21.0 %collective-permute-start.1 = (bf16[128,768]{1,0:T(8,128)(2,1)S(1)}, bf16[128,768]{1,0:T(8,128)(2,1)S(1)}, u32[]{:S(2)}, u32[]{:S(2)}) collective-permute-start(bf16[128,768]{1,0:T(8,128)(2,1)S(1)} %convert_element_type.287), channel_id=1, source_target_pairs={{16,0},{20,4},{24,8},{28,12},{0,16},{4,20},{8,24},{12,28},{17,1},{... | collective-permute-start | bytes 589832 | tf_op jit(solution)/shard_map/ppermute | solution.py:73
  6.9 23.6 %collective-permute-start.2 = (bf16[128,768]{1,0:T(8,128)(2,1)S(1)}, bf16[128,768]{1,0:T(8,128)(2,1)S(1)}, u32[]{:S(2)}, u32[]{:S(2)}) collective-permute-start(bf16[128,768]{1,0:T(8,128)(2,1)S(1)} %convert_element_type.287), channel_id=1, source_target_pairs={{24,0},{28,4},{0,8},{4,12},{8,16},{12,20},{16,24},{20,28},{25,1},{... | collective-permute-start | bytes 589832 | tf_op jit(solution)/shard_map/ppermute | solution.py:73
  8.8 13.3 %collective-permute-start.12 = (bf16[128,256]{1,0:T(8,128)(2,1)S(1)}, bf16[128,256]{1,0:T(8,128)(2,1)S(1)}, u32[]{:S(2)}, u32[]{:S(2)}) collective-permute-start(bf16[128,256]{1,0:T(8,128)(2,1)S(1)} %convert_element_type.293), channel_id=1, source_target_pairs={{8,0},{12,4},{16,8},{20,12},{24,16},{28,20},{0,24},{4,28},{9,1},{1... | collective-permute-start | bytes 196616 | tf_op jit(solution)/shard_map/ppermute | solution.py:73
  12.7 41.1 %collective-permute-start.24 = (bf16[128,1024]{1,0:T(8,128)(2,1)S(1)}, bf16[128,1024]{1,0:T(8,128)(2,1)S(1)}, u32[]{:S(2)}, u32[]{:S(2)}) collective-permute-start(bf16[128,1024]{1,0:T(8,128)(2,1)S(1)} %convert_element_type.295), channel_id=1, source_target_pairs={{8,0},{12,4},{16,8},{20,12},{24,16},{28,20},{0,24},{4,28},{9,1},{1... | collective-permute-start | bytes 786440 | tf_op jit(solution)/shard_map/ppermute | solution.py:73
  22.1 33.3 %collective-permute-start.25 = (bf16[128,1024]{1,0:T(8,128)(2,1)S(1)}, bf16[128,1024]{1,0:T(8,128)(2,1)S(1)}, u32[]{:S(2)}, u32[]{:S(2)}) collective-permute-start(bf16[128,1024]{1,0:T(8,128)(2,1)S(1)} %convert_element_type.295), channel_id=1, source_target_pairs={{16,0},{20,4},{24,8},{28,12},{0,16},{4,20},{8,24},{12,28},{17,1},{... | collective-permute-start | bytes 786440 | tf_op jit(solution)/shard_map/ppermute | solution.py:73
  25.5 29.9 %collective-permute-start.26 = (bf16[128,1024]{1,0:T(8,128)(2,1)S(1)}, bf16[128,1024]{1,0:T(8,128)(2,1)S(1)}, u32[]{:S(2)}, u32[]{:S(2)}) collective-permute-start(bf16[128,1024]{1,0:T(8,128)(2,1)S(1)} %convert_element_type.295), channel_id=1, source_target_pairs={{24,0},{28,4},{0,8},{4,12},{8,16},{12,20},{16,24},{20,28},{25,1},{... | collective-permute-start | bytes 786440 | tf_op jit(solution)/shard_map/ppermute | solution.py:73
  27.9 23.8 %collective-permute-start.13 = (bf16[128,256]{1,0:T(8,128)(2,1)S(1)}, bf16[128,256]{1,0:T(8,128)(2,1)S(1)}, u32[]{:S(2)}, u32[]{:S(2)}) collective-permute-start(bf16[128,256]{1,0:T(8,128)(2,1)S(1)} %convert_element_type.293), channel_id=1, source_target_pairs={{16,0},{20,4},{24,8},{28,12},{0,16},{4,20},{8,24},{12,28},{17,1},{... | collective-permute-start | bytes 196616 | tf_op jit(solution)/shard_map/ppermute | solution.py:73
  30.4 22.8 %collective-permute-start.14 = (bf16[128,256]{1,0:T(8,128)(2,1)S(1)}, bf16[128,256]{1,0:T(8,128)(2,1)S(1)}, u32[]{:S(2)}, u32[]{:S(2)}) collective-permute-start(bf16[128,256]{1,0:T(8,128)(2,1)S(1)} %convert_element_type.293), channel_id=1, source_target_pairs={{24,0},{28,4},{0,8},{4,12},{8,16},{12,20},{16,24},{20,28},{25,1},{... | collective-permute-start | bytes 196616 | tf_op jit(solution)/shard_map/ppermute | solution.py:73
  51.7 56.7 %collective-permute-start.3 = (bf16[4,128,768]{2,1,0:T(8,128)(2,1)S(1)}, bf16[4,128,768]{2,1,0:T(8,128)(2,1)S(1)}, u32[]{:S(2)}, u32[]{:S(2)}) collective-permute-start(bf16[4,128,768]{2,1,0:T(8,128)(2,1)S(1)} %pad_maximum_fusion.7.refs_0_), channel_id=1, source_target_pairs={{0,4},{4,0},{8,12},{12,8},{16,20},{20,16},{24,28},{28,24},{1,5},{5... | collective-permute-start | bytes 2359304 | tf_op jit(solution)/shard_map/ppermute | solution.py:74
  53.2 22.7 %collective-permute-start.15 = (bf16[4,128,256]{2,1,0:T(8,128)(2,1)S(1)}, bf16[4,128,256]{2,1,0:T(8,128)(2,1)S(1)}, u32[]{:S(2)}, u32[]{:S(2)}) collective-permute-start(bf16[4,128,256]{2,1,0:T(8,128)(2,1)S(1)} %pad_maximum_fusion.10.refs_0_), channel_id=1, source_target_pairs={{0,4},{4,0},{8,12},{12,8},{16,20},{20,16},{24,28},{28,24},{1,5},{5... | collective-permute-start | bytes 786440 | tf_op jit(solution)/shard_map/ppermute | solution.py:74
  53.8 23.6 %collective-permute-start.16 = (bf16[4,128,256]{2,1,0:T(8,128)(2,1)S(1)}, bf16[4,128,256]{2,1,0:T(8,128)(2,1)}, u32[]{:S(2)}, u32[]{:S(2)}) collective-permute-start(bf16[4,128,256]{2,1,0:T(8,128)(2,1)S(1)} %pad_maximum_fusion.10.refs_0_), channel_id=1, source_target_pairs={{0,2},{1,3},{2,0},{3,1},{4,6},{5,7},{6,4},{7,5},{8,10},{9,11},{10,... | collective-permute-start | bytes 786440 | tf_op jit(solution)/shard_map/ppermute | solution.py:75
  55.4 23.6 %collective-permute-start.19 = (bf16[4,128,256]{2,1,0:T(8,128)(2,1)S(1)}, bf16[4,128,256]{2,1,0:T(8,128)(2,1)S(1)}, u32[]{:S(2)}, u32[]{:S(2)}) collective-permute-start(bf16[4,128,256]{2,1,0:T(8,128)(2,1)S(1)} %pad_maximum_fusion.10.refs_0_), channel_id=1, source_target_pairs={{0,1},{1,0},{2,3},{3,2},{4,5},{5,4},{6,7},{7,6},{8,9},{9,8},{10,11... | collective-permute-start | bytes 786440 | tf_op jit(solution)/shard_map/ppermute | solution.py:79
  55.4 59.1 %collective-permute-start.4 = (bf16[4,128,768]{2,1,0:T(8,128)(2,1)S(1)}, bf16[4,128,768]{2,1,0:T(8,128)(2,1)}, u32[]{:S(2)}, u32[]{:S(2)}) collective-permute-start(bf16[4,128,768]{2,1,0:T(8,128)(2,1)S(1)} %pad_maximum_fusion.7.refs_0_), channel_id=1, source_target_pairs={{0,2},{1,3},{2,0},{3,1},{4,6},{5,7},{6,4},{7,5},{8,10},{9,11},{10,... | collective-permute-start | bytes 2359304 | tf_op jit(solution)/shard_map/ppermute | solution.py:75
  75.9 48.4 %collective-permute-start.27 = (bf16[4,128,1024]{2,1,0:T(8,128)(2,1)S(1)}, bf16[4,128,1024]{2,1,0:T(8,128)(2,1)S(1)}, u32[]{:S(2)}, u32[]{:S(2)}) collective-permute-start(bf16[4,128,1024]{2,1,0:T(8,128)(2,1)S(1)} %pad_maximum_fusion.1.refs_0_), channel_id=1, source_target_pairs={{0,4},{4,0},{8,12},{12,8},{16,20},{20,16},{24,28},{28,24},{1,5},{5... | collective-permute-start | bytes 3145736 | tf_op jit(solution)/shard_map/ppermute | solution.py:74
  77.4 47.4 %collective-permute-start.28 = (bf16[4,128,1024]{2,1,0:T(8,128)(2,1)S(1)}, bf16[4,128,1024]{2,1,0:T(8,128)(2,1)}, u32[]{:S(2)}, u32[]{:S(2)}) collective-permute-start(bf16[4,128,1024]{2,1,0:T(8,128)(2,1)S(1)} %pad_maximum_fusion.1.refs_0_), channel_id=1, source_target_pairs={{0,2},{1,3},{2,0},{3,1},{4,6},{5,7},{6,4},{7,5},{8,10},{9,11},{10,... | collective-permute-start | bytes 3145736 | tf_op jit(solution)/shard_map/ppermute | solution.py:75
  79.0 24.4 %collective-permute-start.17 = (bf16[2,128,256]{2,1,0:T(8,128)(2,1)S(1)}, bf16[2,128,256]{2,1,0:T(8,128)(2,1)S(1)}, u32[]{:S(2)}, u32[]{:S(2)}) collective-permute-start(bf16[2,128,256]{2,1,0:T(8,128)(2,1)S(1)} %slice.269), channel_id=1, source_target_pairs={{0,2},{1,3},{2,0},{3,1},{4,6},{5,7},{6,4},{7,5},{8,10},{9,11},{10,... | collective-permute-start | bytes 393224 | tf_op jit(solution)/shard_map/ppermute | solution.py:76
  108.3 12.1 %collective-permute-start.20 = (bf16[4,128,256]{2,1,0:T(8,128)(2,1)S(1)}, bf16[4,128,256]{2,1,0:T(8,128)(2,1)}, u32[]{:S(2)}, u32[]{:S(2)}) collective-permute-start(bf16[4,128,256]{2,1,0:T(8,128)(2,1)S(1)} %collective-permute-done.15.refs_1_), channel_id=1, source_target_pairs={{0,1},{1,0},{2,3},{3,2},{4,5},{5,4},{6,7},{7,6},{8,9},{9,8},{10,11... | collective-permute-start | bytes 786440 | tf_op jit(solution)/shard_map/ppermute | solution.py:79
  120.5 11.8 %collective-permute-start.5 = (bf16[2,128,768]{2,1,0:T(8,128)(2,1)}, bf16[2,128,768]{2,1,0:T(8,128)(2,1)}, u32[]{:S(2)}, u32[]{:S(2)}) collective-permute-start(bf16[2,128,768]{2,1,0:T(8,128)(2,1)} %slice.264), channel_id=1, source_target_pairs={{0,2},{1,3},{2,0},{3,1},{4,6},{5,7},{6,4},{7,5},{8,10},{9,11},{10,... | collective-permute-start | bytes 1179656 | tf_op jit(solution)/shard_map/ppermute | solution.py:76
  122.7 11.5 %collective-permute-start.6 = (bf16[2,128,768]{2,1,0:T(8,128)(2,1)}, bf16[2,128,768]{2,1,0:T(8,128)(2,1)}, u32[]{:S(2)}, u32[]{:S(2)}) collective-permute-start(bf16[2,128,768]{2,1,0:T(8,128)(2,1)} %slice.265), channel_id=1, source_target_pairs={{0,4},{4,0},{8,12},{12,8},{16,20},{20,16},{24,28},{28,24},{1,5},{5... | collective-permute-start | bytes 1179656 | tf_op jit(solution)/shard_map/ppermute | solution.py:77
  124.3 17.9 %collective-permute-start.7 = (bf16[4,128,768]{2,1,0:T(8,128)(2,1)S(1)}, bf16[4,128,768]{2,1,0:T(8,128)(2,1)}, u32[]{:S(2)}, u32[]{:S(2)}) collective-permute-start(bf16[4,128,768]{2,1,0:T(8,128)(2,1)S(1)} %pad_maximum_fusion.7.refs_0_), channel_id=1, source_target_pairs={{0,1},{1,0},{2,3},{3,2},{4,5},{5,4},{6,7},{7,6},{8,9},{9,8},{10,11... | collective-permute-start | bytes 2359304 | tf_op jit(solution)/shard_map/ppermute | solution.py:79
  124.3 19.9 %collective-permute-start.8 = (bf16[4,128,768]{2,1,0:T(8,128)(2,1)}, bf16[4,128,768]{2,1,0:T(8,128)(2,1)}, u32[]{:S(2)}, u32[]{:S(2)}) collective-permute-start(bf16[4,128,768]{2,1,0:T(8,128)(2,1)} %copy-done.9), channel_id=1, source_target_pairs={{0,1},{1,0},{2,3},{3,2},{4,5},{5,4},{6,7},{7,6},{8,9},{9,8},{10,11... | collective-permute-start | bytes 2359304 | tf_op jit(solution)/shard_map/ppermute | solution.py:79
  124.8 19.4 %collective-permute-start.9 = (bf16[4,128,768]{2,1,0:T(8,128)(2,1)}, bf16[4,128,768]{2,1,0:T(8,128)(2,1)}, u32[]{:S(2)}, u32[]{:S(2)}) collective-permute-start(bf16[4,128,768]{2,1,0:T(8,128)(2,1)} %collective-permute-done.4.refs_2_), channel_id=1, source_target_pairs={{0,1},{1,0},{2,3},{3,2},{4,5},{5,4},{6,7},{7,6},{8,9},{9,8},{10,11... | collective-permute-start | bytes 2359304 | tf_op jit(solution)/shard_map/ppermute | solution.py:79
  142.2 98.7 %collective-permute-start.31 = (bf16[4,128,1024]{2,1,0:T(8,128)(2,1)S(1)}, bf16[4,128,1024]{2,1,0:T(8,128)(2,1)}, u32[]{:S(2)}, u32[]{:S(2)}) collective-permute-start(bf16[4,128,1024]{2,1,0:T(8,128)(2,1)S(1)} %pad_maximum_fusion.1.refs_0_), channel_id=1, source_target_pairs={{0,1},{1,0},{2,3},{3,2},{4,5},{5,4},{6,7},{7,6},{8,9},{9,8},{10,11... | collective-permute-start | bytes 3145736 | tf_op jit(solution)/shard_map/ppermute | solution.py:79
  142.8 96.7 %collective-permute-start.29 = (bf16[2,128,1024]{2,1,0:T(8,128)(2,1)}, bf16[2,128,1024]{2,1,0:T(8,128)(2,1)S(1)}, u32[]{:S(2)}, u32[]{:S(2)}) collective-permute-start(bf16[2,128,1024]{2,1,0:T(8,128)(2,1)} %slice.271), channel_id=1, source_target_pairs={{0,2},{1,3},{2,0},{3,1},{4,6},{5,7},{6,4},{7,5},{8,10},{9,11},{10,... | collective-permute-start | bytes 1572872 | tf_op jit(solution)/shard_map/ppermute | solution.py:76
  143.3 96.3 %collective-permute-start.30 = (bf16[2,128,1024]{2,1,0:T(8,128)(2,1)}, bf16[2,128,1024]{2,1,0:T(8,128)(2,1)}, u32[]{:S(2)}, u32[]{:S(2)}) collective-permute-start(bf16[2,128,1024]{2,1,0:T(8,128)(2,1)} %slice.272), channel_id=1, source_target_pairs={{0,4},{4,0},{8,12},{12,8},{16,20},{20,16},{24,28},{28,24},{1,5},{5... | collective-permute-start | bytes 1572872 | tf_op jit(solution)/shard_map/ppermute | solution.py:77
  144.2 96.7 %collective-permute-start.32 = (bf16[4,128,1024]{2,1,0:T(8,128)(2,1)S(1)}, bf16[4,128,1024]{2,1,0:T(8,128)(2,1)}, u32[]{:S(2)}, u32[]{:S(2)}) collective-permute-start(bf16[4,128,1024]{2,1,0:T(8,128)(2,1)S(1)} %collective-permute-done.27.refs_1_), channel_id=1, source_target_pairs={{0,1},{1,0},{2,3},{3,2},{4,5},{5,4},{6,7},{7,6},{8,9},{9,8},{10,11... | collective-permute-start | bytes 3145736 | tf_op jit(solution)/shard_map/ppermute | solution.py:79
  144.2 96.7 %collective-permute-start.33 = (bf16[4,128,1024]{2,1,0:T(8,128)(2,1)}, bf16[4,128,1024]{2,1,0:T(8,128)(2,1)}, u32[]{:S(2)}, u32[]{:S(2)}) collective-permute-start(bf16[4,128,1024]{2,1,0:T(8,128)(2,1)} %collective-permute-done.28.refs_2_), channel_id=1, source_target_pairs={{0,1},{1,0},{2,3},{3,2},{4,5},{5,4},{6,7},{7,6},{8,9},{9,8},{10,11... | collective-permute-start | bytes 3145736 | tf_op jit(solution)/shard_map/ppermute | solution.py:79
  322.2 14.0 %collective-permute-start.73 = (bf16[2,512,256]{2,1,0:T(8,128)(2,1)S(1)}, bf16[2,512,256]{2,1,0:T(8,128)(2,1)S(1)}, u32[]{:S(2)}, u32[]{:S(2)}) collective-permute-start(bf16[2,512,256]{2,1,0:T(8,128)(2,1)S(1)} %get-tuple-element.150), channel_id=1, source_target_pairs={{0,2},{1,3},{2,0},{3,1},{4,6},{5,7},{6,4},{7,5},{8,10},{9,11},{10,... | collective-permute-start | bytes 1572872 | tf_op jit(solution)/shard_map/ppermute | solution.py:166
  323.8 13.7 %collective-permute-start.75 = (bf16[2,512,256]{2,1,0:T(8,128)(2,1)S(1)}, bf16[2,512,256]{2,1,0:T(8,128)(2,1)S(1)}, u32[]{:S(2)}, u32[]{:S(2)}) collective-permute-start(bf16[2,512,256]{2,1,0:T(8,128)(2,1)S(1)} %get-tuple-element.151), channel_id=1, source_target_pairs={{0,4},{4,0},{8,12},{12,8},{16,20},{20,16},{24,28},{28,24},{1,5},{5... | collective-permute-start | bytes 1572872 | tf_op jit(solution)/shard_map/ppermute | solution.py:167
  337.9 24.1 %collective-permute-start.74 = (bf16[4,512,256]{2,1,0:T(8,128)(2,1)S(1)}, bf16[4,512,256]{2,1,0:T(8,128)(2,1)S(1)}, u32[]{:S(2)}, u32[]{:S(2)}) collective-permute-start(bf16[4,512,256]{2,1,0:T(8,128)(2,1)S(1)} %pad_maximum_fusion.5), channel_id=1, source_target_pairs={{0,4},{4,0},{8,12},{12,8},{16,20},{20,16},{24,28},{28,24},{1,5},{5... | collective-permute-start | bytes 3145736 | tf_op jit(solution)/shard_map/ppermute | solution.py:170
  339.2 23.8 %collective-permute-start.76 = (bf16[4,512,256]{2,1,0:T(8,128)(2,1)S(1)}, bf16[4,512,256]{2,1,0:T(8,128)(2,1)S(1)}, u32[]{:S(2)}, u32[]{:S(2)}) collective-permute-start(bf16[4,512,256]{2,1,0:T(8,128)(2,1)S(1)} %pad_maximum_fusion.6), channel_id=1, source_target_pairs={{0,2},{1,3},{2,0},{3,1},{4,6},{5,7},{6,4},{7,5},{8,10},{9,11},{10,... | collective-permute-start | bytes 3145736 | tf_op jit(solution)/shard_map/ppermute | solution.py:170
  363.6 19.2 %collective-permute-start.78 = (bf16[512,256]{1,0:T(8,128)(2,1)S(1)}, bf16[512,256]{1,0:T(8,128)(2,1)S(1)}, u32[]{:S(2)}, u32[]{:S(2)}) collective-permute-start(bf16[512,256]{1,0:T(8,128)(2,1)S(1)} %get-tuple-element.168), channel_id=1, source_target_pairs={{0,16},{4,20},{8,24},{12,28},{16,0},{20,4},{24,8},{28,12},{1,17},{... | collective-permute-start | bytes 786440 | tf_op jit(solution)/shard_map/ppermute | solution.py:173
  366.1 16.8 %collective-permute-start.79 = (bf16[512,256]{1,0:T(8,128)(2,1)S(1)}, bf16[512,256]{1,0:T(8,128)(2,1)S(1)}, u32[]{:S(2)}, u32[]{:S(2)}) collective-permute-start(bf16[512,256]{1,0:T(8,128)(2,1)S(1)} %get-tuple-element.167), channel_id=1, source_target_pairs={{0,24},{4,28},{8,0},{12,4},{16,8},{20,12},{24,16},{28,20},{1,25},{... | collective-permute-start | bytes 786440 | tf_op jit(solution)/shard_map/ppermute | solution.py:173
  384.4 13.0 %collective-permute-start.36 = (bf16[512,256]{1,0:T(8,128)(2,1)S(1)}, bf16[512,256]{1,0:T(8,128)(2,1)S(1)}, u32[]{:S(2)}, u32[]{:S(2)}) collective-permute-start(bf16[512,256]{1,0:T(8,128)(2,1)S(1)} %get-tuple-element.179), channel_id=1, source_target_pairs={{8,0},{12,4},{16,8},{20,12},{24,16},{28,20},{0,24},{4,28},{9,1},{1... | collective-permute-start | bytes 786440 | tf_op jit(solution)/shard_map/ppermute | solution.py:73
  390.6 22.6 %collective-permute-start.37 = (bf16[512,256]{1,0:T(8,128)(2,1)S(1)}, bf16[512,256]{1,0:T(8,128)(2,1)S(1)}, u32[]{:S(2)}, u32[]{:S(2)}) collective-permute-start(bf16[512,256]{1,0:T(8,128)(2,1)S(1)} %get-tuple-element.179), channel_id=1, source_target_pairs={{16,0},{20,4},{24,8},{28,12},{0,16},{4,20},{8,24},{12,28},{17,1},{... | collective-permute-start | bytes 786440 | tf_op jit(solution)/shard_map/ppermute | solution.py:73
  391.1 22.2 %collective-permute-start.38 = (bf16[512,256]{1,0:T(8,128)(2,1)S(1)}, bf16[512,256]{1,0:T(8,128)(2,1)S(1)}, u32[]{:S(2)}, u32[]{:S(2)}) collective-permute-start(bf16[512,256]{1,0:T(8,128)(2,1)S(1)} %get-tuple-element.179), channel_id=1, source_target_pairs={{24,0},{28,4},{0,8},{4,12},{8,16},{12,20},{16,24},{20,28},{25,1},{... | collective-permute-start | bytes 786440 | tf_op jit(solution)/shard_map/ppermute | solution.py:73
  413.4 23.3 %collective-permute-start.39 = (bf16[4,512,256]{2,1,0:T(8,128)(2,1)S(1)}, bf16[4,512,256]{2,1,0:T(8,128)(2,1)S(1)}, u32[]{:S(2)}, u32[]{:S(2)}) collective-permute-start(bf16[4,512,256]{2,1,0:T(8,128)(2,1)S(1)} %pad_maximum_fusion.2.refs_0_), channel_id=1, source_target_pairs={{0,4},{4,0},{8,12},{12,8},{16,20},{20,16},{24,28},{28,24},{1,5},{5... | collective-permute-start | bytes 3145736 | tf_op jit(solution)/shard_map/ppermute | solution.py:74
  414.5 23.9 %collective-permute-start.40 = (bf16[4,512,256]{2,1,0:T(8,128)(2,1)S(1)}, bf16[4,512,256]{2,1,0:T(8,128)(2,1)S(1)}, u32[]{:S(2)}, u32[]{:S(2)}) collective-permute-start(bf16[4,512,256]{2,1,0:T(8,128)(2,1)S(1)} %pad_maximum_fusion.2.refs_0_), channel_id=1, source_target_pairs={{0,2},{1,3},{2,0},{3,1},{4,6},{5,7},{6,4},{7,5},{8,10},{9,11},{10,... | collective-permute-start | bytes 3145736 | tf_op jit(solution)/shard_map/ppermute | solution.py:75
  415.2 41.9 %collective-permute-start.43 = (bf16[4,512,256]{2,1,0:T(8,128)(2,1)S(1)}, bf16[4,512,256]{2,1,0:T(8,128)(2,1)}, u32[]{:S(2)}, u32[]{:S(2)}) collective-permute-start(bf16[4,512,256]{2,1,0:T(8,128)(2,1)S(1)} %pad_maximum_fusion.2.refs_0_), channel_id=1, source_target_pairs={{0,1},{1,0},{2,3},{3,2},{4,5},{5,4},{6,7},{7,6},{8,9},{9,8},{10,11... | collective-permute-start | bytes 3145736 | tf_op jit(solution)/shard_map/ppermute | solution.py:79
  436.8 12.1 %collective-permute-start.41 = (bf16[2,512,256]{2,1,0:T(8,128)(2,1)S(1)}, bf16[2,512,256]{2,1,0:T(8,128)(2,1)}, u32[]{:S(2)}, u32[]{:S(2)}) collective-permute-start(bf16[2,512,256]{2,1,0:T(8,128)(2,1)S(1)} %slice.273), channel_id=1, source_target_pairs={{0,2},{1,3},{2,0},{3,1},{4,6},{5,7},{6,4},{7,5},{8,10},{9,11},{10,... | collective-permute-start | bytes 1572872 | tf_op jit(solution)/shard_map/ppermute | solution.py:76
  437.5 19.6 %collective-permute-start.44 = (bf16[4,512,256]{2,1,0:T(8,128)(2,1)S(1)}, bf16[4,512,256]{2,1,0:T(8,128)(2,1)}, u32[]{:S(2)}, u32[]{:S(2)}) collective-permute-start(bf16[4,512,256]{2,1,0:T(8,128)(2,1)S(1)} %collective-permute-done.39.refs_1_), channel_id=1, source_target_pairs={{0,1},{1,0},{2,3},{3,2},{4,5},{5,4},{6,7},{7,6},{8,9},{9,8},{10,11... | collective-permute-start | bytes 3145736 | tf_op jit(solution)/shard_map/ppermute | solution.py:79
  438.4 18.7 %collective-permute-start.45 = (bf16[4,512,256]{2,1,0:T(8,128)(2,1)S(1)}, bf16[4,512,256]{2,1,0:T(8,128)(2,1)}, u32[]{:S(2)}, u32[]{:S(2)}) collective-permute-start(bf16[4,512,256]{2,1,0:T(8,128)(2,1)S(1)} %collective-permute-done.40.refs_2_), channel_id=1, source_target_pairs={{0,1},{1,0},{2,3},{3,2},{4,5},{5,4},{6,7},{7,6},{8,9},{9,8},{10,11... | collective-permute-start | bytes 3145736 | tf_op jit(solution)/shard_map/ppermute | solution.py:79
  438.5 14.4 %collective-permute-start.42 = (bf16[2,512,256]{2,1,0:T(8,128)(2,1)S(1)}, bf16[2,512,256]{2,1,0:T(8,128)(2,1)}, u32[]{:S(2)}, u32[]{:S(2)}) collective-permute-start(bf16[2,512,256]{2,1,0:T(8,128)(2,1)S(1)} %slice.274), channel_id=1, source_target_pairs={{0,4},{4,0},{8,12},{12,8},{16,20},{20,16},{24,28},{28,24},{1,5},{5... | collective-permute-start | bytes 1572872 | tf_op jit(solution)/shard_map/ppermute | solution.py:77
  658.7 78.4 %collective-permute-start.64 = (bf16[2,2,4,128,1024]{4,3,2,1,0:T(8,128)(2,1)}, bf16[2,2,4,128,1024]{4,3,2,1,0:T(8,128)(2,1)}, u32[]{:S(2)}, u32[]{:S(2)}) collective-permute-start(bf16[2,2,4,128,1024]{4,3,2,1,0:T(8,128)(2,1)} %get-tuple-element.39), channel_id=1, source_target_pairs={{0,1},{1,0},{2,3},{3,2},{4,5},{5,4},{6,7},{7,6},{8,9},{9,8},{10,11... | collective-permute-start | bytes 12582920 | tf_op jit(solution)/shard_map/ppermute | solution.py:165
  665.9 62.3 %collective-permute-start.48 = (bf16[2,2,4,128,768]{4,3,2,1,0:T(8,128)(2,1)}, bf16[2,2,4,128,768]{4,3,2,1,0:T(8,128)(2,1)}, u32[]{:S(2)}, u32[]{:S(2)}) collective-permute-start(bf16[2,2,4,128,768]{4,3,2,1,0:T(8,128)(2,1)} %get-tuple-element.35), channel_id=1, source_target_pairs={{0,1},{1,0},{2,3},{3,2},{4,5},{5,4},{6,7},{7,6},{8,9},{9,8},{10,11... | collective-permute-start | bytes 9437192 | tf_op jit(solution)/shard_map/ppermute | solution.py:165
  675.8 45.9 %collective-permute-start.58 = (bf16[4,128,256]{2,1,0:T(8,128)(2,1)}, bf16[4,128,256]{2,1,0:T(8,128)(2,1)S(1)}, u32[]{:S(2)}, u32[]{:S(2)}) collective-permute-start(bf16[4,128,256]{2,1,0:T(8,128)(2,1)} %pad_maximum_fusion.11), channel_id=1, source_target_pairs={{0,4},{4,0},{8,12},{12,8},{16,20},{20,16},{24,28},{28,24},{1,5},{5... | collective-permute-start | bytes 786440 | tf_op jit(solution)/shard_map/ppermute | solution.py:170
  677.5 44.2 %collective-permute-start.60 = (bf16[4,128,256]{2,1,0:T(8,128)(2,1)}, bf16[4,128,256]{2,1,0:T(8,128)(2,1)}, u32[]{:S(2)}, u32[]{:S(2)}) collective-permute-start(bf16[4,128,256]{2,1,0:T(8,128)(2,1)} %pad_maximum_fusion.12), channel_id=1, source_target_pairs={{0,2},{1,3},{2,0},{3,1},{4,6},{5,7},{6,4},{7,5},{8,10},{9,11},{10,... | collective-permute-start | bytes 786440 | tf_op jit(solution)/shard_map/ppermute | solution.py:170
  724.4 41.0 %collective-permute-start.61 = (bf16[128,256]{1,0:T(8,128)(2,1)}, bf16[128,256]{1,0:T(8,128)(2,1)S(1)}, u32[]{:S(2)}, u32[]{:S(2)}) collective-permute-start(bf16[128,256]{1,0:T(8,128)(2,1)} %get-tuple-element.180), channel_id=1, source_target_pairs={{0,8},{4,12},{8,16},{12,20},{16,24},{20,28},{24,0},{28,4},{1,9},{5... | collective-permute-start | bytes 196616 | tf_op jit(solution)/shard_map/ppermute | solution.py:173
  724.7 41.0 %collective-permute-start.62 = (bf16[128,256]{1,0:T(8,128)(2,1)}, bf16[128,256]{1,0:T(8,128)(2,1)}, u32[]{:S(2)}, u32[]{:S(2)}) collective-permute-start(bf16[128,256]{1,0:T(8,128)(2,1)} %get-tuple-element.182), channel_id=1, source_target_pairs={{0,16},{4,20},{8,24},{12,28},{16,0},{20,4},{24,8},{28,12},{1,17},{... | collective-permute-start | bytes 196616 | tf_op jit(solution)/shard_map/ppermute | solution.py:173
  727.2 47.9 %collective-permute-start.63 = (bf16[128,256]{1,0:T(8,128)(2,1)}, bf16[128,256]{1,0:T(8,128)(2,1)}, u32[]{:S(2)}, u32[]{:S(2)}) collective-permute-start(bf16[128,256]{1,0:T(8,128)(2,1)} %get-tuple-element.181), channel_id=1, source_target_pairs={{0,24},{4,28},{8,0},{12,4},{16,8},{20,12},{24,16},{28,20},{1,25},{... | collective-permute-start | bytes 196616 | tf_op jit(solution)/shard_map/ppermute | solution.py:173
  734.7 13.0 %collective-permute-start.49 = (bf16[2,128,768]{2,1,0:T(8,128)(2,1)}, bf16[2,128,768]{2,1,0:T(8,128)(2,1)S(1)}, u32[]{:S(2)}, u32[]{:S(2)}) collective-permute-start(bf16[2,128,768]{2,1,0:T(8,128)(2,1)} %get-tuple-element.158), channel_id=1, source_target_pairs={{0,2},{1,3},{2,0},{3,1},{4,6},{5,7},{6,4},{7,5},{8,10},{9,11},{10,... | collective-permute-start | bytes 1179656 | tf_op jit(solution)/shard_map/ppermute | solution.py:166
  737.0 11.8 %collective-permute-start.51 = (bf16[2,128,768]{2,1,0:T(8,128)(2,1)S(1)}, bf16[2,128,768]{2,1,0:T(8,128)(2,1)S(1)}, u32[]{:S(2)}, u32[]{:S(2)}) collective-permute-start(bf16[2,128,768]{2,1,0:T(8,128)(2,1)S(1)} %get-tuple-element.159), channel_id=1, source_target_pairs={{0,4},{4,0},{8,12},{12,8},{16,20},{20,16},{24,28},{28,24},{1,5},{5... | collective-permute-start | bytes 1179656 | tf_op jit(solution)/shard_map/ppermute | solution.py:167
  747.7 11.9 %collective-permute-start.65 = (bf16[2,128,1024]{2,1,0:T(8,128)(2,1)S(1)}, bf16[2,128,1024]{2,1,0:T(8,128)(2,1)S(1)}, u32[]{:S(2)}, u32[]{:S(2)}) collective-permute-start(bf16[2,128,1024]{2,1,0:T(8,128)(2,1)S(1)} %get-tuple-element.154), channel_id=1, source_target_pairs={{0,2},{1,3},{2,0},{3,1},{4,6},{5,7},{6,4},{7,5},{8,10},{9,11},{10,... | collective-permute-start | bytes 1572872 | tf_op jit(solution)/shard_map/ppermute | solution.py:166
  748.8 11.6 %collective-permute-start.67 = (bf16[2,128,1024]{2,1,0:T(8,128)(2,1)S(1)}, bf16[2,128,1024]{2,1,0:T(8,128)(2,1)S(1)}, u32[]{:S(2)}, u32[]{:S(2)}) collective-permute-start(bf16[2,128,1024]{2,1,0:T(8,128)(2,1)S(1)} %get-tuple-element.155), channel_id=1, source_target_pairs={{0,4},{4,0},{8,12},{12,8},{16,20},{20,16},{24,28},{28,24},{1,5},{5... | collective-permute-start | bytes 1572872 | tf_op jit(solution)/shard_map/ppermute | solution.py:167
  759.6 20.8 %collective-permute-start.50 = (bf16[4,128,768]{2,1,0:T(8,128)(2,1)}, bf16[4,128,768]{2,1,0:T(8,128)(2,1)}, u32[]{:S(2)}, u32[]{:S(2)}) collective-permute-start(bf16[4,128,768]{2,1,0:T(8,128)(2,1)} %pad_maximum_fusion.8), channel_id=1, source_target_pairs={{0,4},{4,0},{8,12},{12,8},{16,20},{20,16},{24,28},{28,24},{1,5},{5... | collective-permute-start | bytes 2359304 | tf_op jit(solution)/shard_map/ppermute | solution.py:170
  760.4 21.2 %collective-permute-start.52 = (bf16[4,128,768]{2,1,0:T(8,128)(2,1)}, bf16[4,128,768]{2,1,0:T(8,128)(2,1)}, u32[]{:S(2)}, u32[]{:S(2)}) collective-permute-start(bf16[4,128,768]{2,1,0:T(8,128)(2,1)} %pad_maximum_fusion.9), channel_id=1, source_target_pairs={{0,2},{1,3},{2,0},{3,1},{4,6},{5,7},{6,4},{7,5},{8,10},{9,11},{10,... | collective-permute-start | bytes 2359304 | tf_op jit(solution)/shard_map/ppermute | solution.py:170
  765.4 33.4 %collective-permute-start.66 = (bf16[4,128,1024]{2,1,0:T(8,128)(2,1)}, bf16[4,128,1024]{2,1,0:T(8,128)(2,1)S(1)}, u32[]{:S(2)}, u32[]{:S(2)}) collective-permute-start(bf16[4,128,1024]{2,1,0:T(8,128)(2,1)} %pad_maximum_fusion.3), channel_id=1, source_target_pairs={{0,4},{4,0},{8,12},{12,8},{16,20},{20,16},{24,28},{28,24},{1,5},{5... | collective-permute-start | bytes 3145736 | tf_op jit(solution)/shard_map/ppermute | solution.py:170
  765.8 33.1 %collective-permute-start.68 = (bf16[4,128,1024]{2,1,0:T(8,128)(2,1)}, bf16[4,128,1024]{2,1,0:T(8,128)(2,1)}, u32[]{:S(2)}, u32[]{:S(2)}) collective-permute-start(bf16[4,128,1024]{2,1,0:T(8,128)(2,1)} %pad_maximum_fusion.4), channel_id=1, source_target_pairs={{0,2},{1,3},{2,0},{3,1},{4,6},{5,7},{6,4},{7,5},{8,10},{9,11},{10,... | collective-permute-start | bytes 3145736 | tf_op jit(solution)/shard_map/ppermute | solution.py:170
  783.8 19.5 %collective-permute-start.53 = (bf16[128,768]{1,0:T(8,128)(2,1)S(1)}, bf16[128,768]{1,0:T(8,128)(2,1)S(1)}, u32[]{:S(2)}, u32[]{:S(2)}) collective-permute-start(bf16[128,768]{1,0:T(8,128)(2,1)S(1)} %get-tuple-element.176), channel_id=1, source_target_pairs={{0,8},{4,12},{8,16},{12,20},{16,24},{20,28},{24,0},{28,4},{1,9},{5... | collective-permute-start | bytes 589832 | tf_op jit(solution)/shard_map/ppermute | solution.py:173
  784.9 21.3 %collective-permute-start.54 = (bf16[128,768]{1,0:T(8,128)(2,1)S(1)}, bf16[128,768]{1,0:T(8,128)(2,1)S(1)}, u32[]{:S(2)}, u32[]{:S(2)}) collective-permute-start(bf16[128,768]{1,0:T(8,128)(2,1)S(1)} %get-tuple-element.178), channel_id=1, source_target_pairs={{0,16},{4,20},{8,24},{12,28},{16,0},{20,4},{24,8},{28,12},{1,17},{... | collective-permute-start | bytes 589832 | tf_op jit(solution)/shard_map/ppermute | solution.py:173
  786.5 19.7 %collective-permute-start.55 = (bf16[128,768]{1,0:T(8,128)(2,1)S(1)}, bf16[128,768]{1,0:T(8,128)(2,1)S(1)}, u32[]{:S(2)}, u32[]{:S(2)}) collective-permute-start(bf16[128,768]{1,0:T(8,128)(2,1)S(1)} %get-tuple-element.177), channel_id=1, source_target_pairs={{0,24},{4,28},{8,0},{12,4},{16,8},{20,12},{24,16},{28,20},{1,25},{... | collective-permute-start | bytes 589832 | tf_op jit(solution)/shard_map/ppermute | solution.py:173
  802.3 17.0 %collective-permute-start.70 = (bf16[128,1024]{1,0:T(8,128)(2,1)S(1)}, bf16[128,1024]{1,0:T(8,128)(2,1)S(1)}, u32[]{:S(2)}, u32[]{:S(2)}) collective-permute-start(bf16[128,1024]{1,0:T(8,128)(2,1)S(1)} %get-tuple-element.171), channel_id=1, source_target_pairs={{0,16},{4,20},{8,24},{12,28},{16,0},{20,4},{24,8},{28,12},{1,17},{... | collective-permute-start | bytes 786440 | tf_op jit(solution)/shard_map/ppermute | solution.py:173
  803.4 15.9 %collective-permute-start.71 = (bf16[128,1024]{1,0:T(8,128)(2,1)S(1)}, bf16[128,1024]{1,0:T(8,128)(2,1)S(1)}, u32[]{:S(2)}, u32[]{:S(2)}) collective-permute-start(bf16[128,1024]{1,0:T(8,128)(2,1)S(1)} %get-tuple-element.170), channel_id=1, source_target_pairs={{0,24},{4,28},{8,0},{12,4},{16,8},{20,12},{24,16},{28,20},{1,25},{... | collective-permute-start | bytes 786440 | tf_op jit(solution)/shard_map/ppermute | solution.py:173
  (114 other events, 1360.5 us)
